TPU v7x, 32 devices: a whole 2x2x4 slice. The times are simulated.
32 devices in a mesh: section: 4 (over y, x), row: 4 (over z), col: 2 (over core).
Axes of the slice: x: 2, y: 2, z: 4, core: 2. Of those that a mesh axis runs over, the one named last changes fastest.
Arguments:
- section_inputs: bfloat16 [4, 512, 2048], P('section', 'col', 'row'), may hold values from -6 to 6
- out_grad: bfloat16 [4, 512, 2048], P('section', 'col', 'row'), may hold values from -6 to 6
- saved_gate: bfloat16 [4, 512, 8192], P('section', 'row', 'col'), may hold values from -6 to 6
- saved_up: bfloat16 [4, 512, 8192], P('section', 'row', 'col'), may hold values from -6 to 6
- gate_weight: bfloat16 [4, 2048, 8192], P('section', 'row', 'col'), may hold values from -0.125 to 0.125
- up_weight: bfloat16 [4, 2048, 8192], P('section', 'row', 'col'), may hold values from -0.125 to 0.125
- down_weight: bfloat16 [4, 8192, 2048], P('section', 'col', 'row'), may hold values from -0.0625 to 0.0625
- momentum_gate: float32 [4, 2048, 8192], P('section', 'row', 'col'), may hold values from -6 to 6
- momentum_up: float32 [4, 2048, 8192], P('section', 'row', 'col'), may hold values from -6 to 6
- momentum_down: float32 [4, 8192, 2048], P('section', 'col', 'row'), may hold values from -6 to 6
- noise_gate: bfloat16 [4, 2048, 8192], P('section', 'row', 'col'), may hold values from -6 to 6
- noise_up: bfloat16 [4, 2048, 8192], P('section', 'row', 'col'), may hold values from -6 to 6
- noise_down: bfloat16 [4, 8192, 2048], P('section', 'col', 'row'), may hold values from -6 to 6
Outputs:
- prev_grads: bfloat16 [4, 512, 2048], P('section', 'col', 'row')
- new_gate: bfloat16 [4, 2048, 8192], P('section', 'row', 'col')
- new_up: bfloat16 [4, 2048, 8192], P('section', 'row', 'col')
- new_down: bfloat16 [4, 8192, 2048], P('section', 'col', 'row')
- next_momentum_gate: float32 [4, 2048, 8192], P('section', 'row', 'col')
- next_momentum_up: float32 [4, 2048, 8192], P('section', 'row', 'col')
- next_momentum_down: float32 [4, 8192, 2048], P('section', 'col', 'row')
All inputs are finite; a program needn't handle non-finite values.
Results may differ from a plain program's by a relative error of at most 0.025.
Values may be sent and summed in bfloat16 or wider, within the bound.
No kernel may reach another device: no remote copies, remote signals or barrier semaphores. Data moves between devices by JAX's collectives and lax.ppermute only.
A program may use at most 192 MiB of HBM per device.

v0:
```python
import jax
import jax.numpy as jnp
from jax import lax
from jax.sharding import PartitionSpec as P

FRICTION = 0.1
DRIFT = 0.01


def from_behind(shard, axis, by):
    size = lax.axis_size(axis)
    pairs = [(i, i + by) for i in range(size) if 0 <= i + by < size]
    return lax.ppermute(shard, axis, pairs)


def contract(left, right, left_dim, right_dim):
    return lax.dot_general(
        left, right, (((left_dim,), (right_dim,)), ((), ())), preferred_element_type=jnp.float32
    )


def pre_grads(hidden_grad, gate_pre, up_pre):
    gate_wide = gate_pre.astype(jnp.float32)
    up_wide = up_pre.astype(jnp.float32)
    sigmoid_gate = jax.nn.sigmoid(gate_wide)
    silu_gate = gate_wide * sigmoid_gate
    slope = sigmoid_gate * (1.0 + gate_wide * (1.0 - sigmoid_gate))
    gate_grad = (hidden_grad * up_wide * slope).astype(jnp.bfloat16)
    up_grad = (hidden_grad * silu_gate).astype(jnp.bfloat16)
    hidden_saved = (silu_gate * up_wide).astype(jnp.bfloat16)
    return (hidden_saved, gate_grad, up_grad)


def sghmc_step(weight, momentum, gradient, noise, kick_scale):
    moved = (
        (1.0 - FRICTION) * momentum
        - kick_scale * gradient
        + (2.0 * FRICTION) ** 0.5 * noise.astype(jnp.float32)
    )
    fresh = (weight.astype(jnp.float32) + DRIFT * moved).astype(jnp.bfloat16)
    return (fresh[None], moved[None])


def shards(
    section_inputs,
    out_grad,
    saved_gate,
    saved_up,
    gate_weight,
    up_weight,
    down_weight,
    momentum_gate,
    momentum_up,
    momentum_down,
    noise_gate,
    noise_up,
    noise_down,
):
    inputs_full, grads_full = (
        lax.all_gather(section_inputs[0], "col", axis=0, tiled=True),
        lax.all_gather(out_grad[0], "col", axis=0, tiled=True),
    )
    tokens = inputs_full.shape[0]
    gate_local = gate_weight[0]
    up_local = up_weight[0]
    down_local = down_weight[0]
    grad_block = grads_full
    hidden_grad = lax.psum_scatter(
        contract(grad_block, down_local, 1, 1).astype(jnp.bfloat16),
        "row",
        scatter_dimension=0,
        tiled=True,
    ).astype(jnp.float32)
    hidden_saved, gate_grad, up_grad = pre_grads(hidden_grad, saved_gate[0], saved_up[0])
    hidden_piece = lax.all_gather(hidden_saved, "row", axis=0, tiled=True)
    gate_piece = lax.all_gather(gate_grad, "row", axis=0, tiled=True)
    up_piece = lax.all_gather(up_grad, "row", axis=0, tiled=True)
    grad_block = grads_full
    down_total = contract(hidden_piece, grad_block, 0, 0)
    gate_total = contract(inputs_full, gate_piece, 0, 0)
    up_total = contract(inputs_full, up_piece, 0, 0)
    partial_value = contract(gate_piece, gate_local, 1, 1) + contract(up_piece, up_local, 1, 1)
    input_part = partial_value
    down_wgrad, gate_wgrad, up_wgrad, input_part = (down_total, gate_total, up_total, input_part)
    input_grad = lax.psum_scatter(
        input_part.astype(jnp.bfloat16), "col", scatter_dimension=0, tiled=True
    )
    passed = from_behind(input_grad, "section", -1)
    kick_scale = float(tokens) ** (-0.5)
    new_gate, next_gate = sghmc_step(
        gate_local, momentum_gate[0], gate_wgrad, noise_gate[0], kick_scale
    )
    new_up, next_up = sghmc_step(up_local, momentum_up[0], up_wgrad, noise_up[0], kick_scale)
    new_down, next_down = sghmc_step(
        down_local, momentum_down[0], down_wgrad, noise_down[0], kick_scale
    )
    return (passed[None], new_gate, new_up, new_down, next_gate, next_up, next_down)


def solution(mesh):
    in_specs = (
        P("section", "col", "row"),
        P("section", "col", "row"),
        P("section", "row", "col"),
        P("section", "row", "col"),
        P("section", "row", "col"),
        P("section", "row", "col"),
        P("section", "col", "row"),
        P("section", "row", "col"),
        P("section", "row", "col"),
        P("section", "col", "row"),
        P("section", "row", "col"),
        P("section", "row", "col"),
        P("section", "col", "row"),
    )
    out_specs = (
        P("section", "col", "row"),
        P("section", "row", "col"),
        P("section", "row", "col"),
        P("section", "col", "row"),
        P("section", "row", "col"),
        P("section", "row", "col"),
        P("section", "col", "row"),
    )
    return jax.shard_map(shards, mesh=mesh, in_specs=in_specs, out_specs=out_specs, check_vma=False)
```

profile of v0, /device:TPU:10, one launch (start us, length us, event | category | flops | bytes accessed | tf_op | source)
XLA Modules:
  0.0 436.6 jit_solution(16233494224309320577)
XLA Ops:
  9.6 6.6 %convolution_convert_fusion = bf16[512,4096]{1,0:T(8,128)(2,1)} fusion(bf16[1,4096,512]{2,1,0:T(8,128)(2,1)} %param.19, bf16[1,512,512]{2,1,0:T(8,128)(2,1)S(1)} %all-gather), kind=kOutput, calls=%fused_computation.9 | convolution fusion | flops 2149580800 | bytes 8912896 | tf_op jit(solution)/shard_map/dot_general | solution.py:17
  16.3 78.0 %reduce-scatter.3.cloned.1.call-done = bf16[128,4096]{1,0:T(8,128)(2,1)} async-done(((bf16[512,4096]{1,0:T(8,128)(2,1)}), bf16[128,4096]{1,0:T(8,128)(2,1)}) %reduce-scatter.3.cloned.1.call-update) | async-done | bytes 1048592 | tf_op jit(solution)/shard_map/reduce_scatter | solution.py:68
  94.3 4.1 fusion.11
  99.8 9.1 %copy.22 = f32[1,512,4096]{1,2,0:T(8,128)} copy(f32[1,512,4096]{2,1,0:T(8,128)} %param.20) | data formatting | bytes 16777216 | tf_op args[7]
  108.9 6.5 %copy.23 = bf16[1,512,4096]{1,2,0:T(8,128)(2,1)} copy(bf16[1,512,4096]{2,1,0:T(8,128)(2,1)} %param.23) | data formatting | bytes 8388608 | tf_op args[10]
  115.3 6.4 %copy.20 = bf16[1,512,4096]{1,2,0:T(8,128)(2,1)} copy(bf16[1,512,4096]{2,1,0:T(8,128)(2,1)} %param.17) | data formatting | bytes 8388608 | tf_op args[4]
  121.7 9.0 %copy.24 = f32[1,512,4096]{1,2,0:T(8,128)} copy(f32[1,512,4096]{2,1,0:T(8,128)} %param.21) | data formatting | bytes 16777216 | tf_op args[8]
  130.7 6.5 %copy.25 = bf16[1,512,4096]{1,2,0:T(8,128)(2,1)} copy(bf16[1,512,4096]{2,1,0:T(8,128)(2,1)} %param.24) | data formatting | bytes 8388608 | tf_op args[11]
  137.2 6.5 %copy.21 = bf16[1,512,4096]{1,2,0:T(8,128)(2,1)} copy(bf16[1,512,4096]{2,1,0:T(8,128)(2,1)} %param.18) | data formatting | bytes 8388608 | tf_op args[5]
  146.1 31.3 %all-gather.8.cloned.1.call-done = bf16[512,4096]{1,0:T(8,128)(2,1)} async-done(((bf16[128,4096]{1,0:T(8,128)(2,1)}), bf16[512,4096]{1,0:T(8,128)(2,1)}) %all-gather.8.cloned.1.call-update) | async-done | bytes 4194320 | tf_op jit(solution)/shard_map/all_gather | solution.py:77
  177.4 5.8 %fusion.3 = f32[512,512]{1,0:T(8,128)S(1)} fusion(bf16[512,4096]{1,0:T(8,128)(2,1)} %all-gather.8.cloned.1.call-done, bf16[1,512,4096]{2,1,0:T(8,128)(2,1)} %param.18), kind=kOutput, calls=%fused_computation.13 | convolution fusion | flops 2147483648 | bytes 9437184 | tf_op jit(solution)/shard_map/dot_general | solution.py:17
  183.2 75.7 %all-gather.6.cloned.1.call-done = bf16[512,4096]{1,0:T(8,128)(2,1)} async-done(((bf16[128,4096]{1,0:T(8,128)(2,1)}), bf16[512,4096]{1,0:T(8,128)(2,1)}) %all-gather.6.cloned.1.call-update) | async-done | bytes 4194320 | tf_op jit(solution)/shard_map/all_gather | solution.py:76
  258.9 6.6 %fusion.20 = bf16[512,512]{1,0:T(8,128)(2,1)} fusion(f32[512,512]{1,0:T(8,128)S(1)} %fusion.3, bf16[512,4096]{1,0:T(8,128)(2,1)} %all-gather.6.cloned.1.call-done, bf16[1,512,4096]{2,1,0:T(8,128)(2,1)} %param.17), kind=kOutput, calls=%fused_computation.34 | convolution fusion | flops 2148007936 | bytes 9961472 | tf_op jit(solution)/shard_map/dot_general | solution.py:17
  265.6 74.7 %all-gather.10.cloned.1.call-done = bf16[512,4096]{1,0:T(8,128)(2,1)} async-done(((bf16[128,4096]{1,0:T(8,128)(2,1)}), bf16[512,4096]{1,0:T(8,128)(2,1)}) %all-gather.10.cloned.1.call-update) | async-done | bytes 4194320 | tf_op jit(solution)/shard_map/all_gather | solution.py:75
  340.3 9.7 %bitcast_add_fusion = f32[4096,512]{1,0:T(8,128)S(1)} fusion(bf16[1,4096,512]{2,1,0:T(8,128)(2,1)} %param.25, f32[1,4096,512]{2,1,0:T(8,128)} %param.22, bf16[512,4096]{1,0:T(8,128)(2,1)} %all-gather.10.cloned.1.call-done, bf16[1,512,512]{2,1,0:T(8,128)(2,1)S(1)} %all-gather), kind=kOutput, calls=%fused_computation | convolution fusion | flops 2160066560 | bytes 25690112 | tf_op jit(solution)/shard_map/dot_general | solution.py:17
  353.5 5.8 %fusion.2 = bf16[1,4096,512]{2,1,0:T(8,128)(2,1)} fusion(f32[4096,512]{1,0:T(8,128)S(1)} %bitcast_add_fusion, bf16[1,4096,512]{2,1,0:T(8,128)(2,1)} %param.19), kind=kLoop, calls=%fused_computation.12 | loop fusion | flops 8388608 | bytes 16777216 | tf_op jit(solution)/shard_map/broadcast_in_dim | solution.py:41
  359.3 8.7 %bitcast_add_fusion.2 = f32[512,4096]{0,1:T(8,128)S(1)} fusion(bf16[1,512,4096]{1,2,0:T(8,128)(2,1)S(1)} %copy-done.3, f32[1,512,4096]{1,2,0:T(8,128)} %copy.22, bf16[512,4096]{1,0:T(8,128)(2,1)} %all-gather.6.cloned.1.call-done, bf16[1,512,512]{2,1,0:T(8,128)(2,1)S(1)} %all-gather.1), kind=kOutput, calls=%fused_computation.4 | convolution fusion | flops 2160066560 | bytes 25690112 | tf_op jit(solution)/shard_map/dot_general | solution.py:17
  368.1 8.7 %fusion = bf16[1,512,4096]{1,2,0:T(8,128)(2,1)} fusion(f32[512,4096]{0,1:T(8,128)S(1)} %bitcast_add_fusion.2, bf16[1,512,4096]{1,2,0:T(8,128)(2,1)} %copy.20), kind=kLoop, calls=%fused_computation.10 | loop fusion | flops 8388608 | bytes 16777216 | tf_op jit(solution)/shard_map/broadcast_in_dim | solution.py:41
  376.8 11.8 %bitcast_add_fusion.1 = f32[512,4096]{0,1:T(8,128)} fusion(bf16[1,512,4096]{1,2,0:T(8,128)(2,1)S(1)} %copy-done.2, f32[1,512,4096]{1,2,0:T(8,128)} %copy.24, bf16[512,4096]{1,0:T(8,128)(2,1)} %all-gather.8.cloned.1.call-done, bf16[1,512,512]{2,1,0:T(8,128)(2,1)S(1)} %all-gather.1), kind=kOutput, calls=%fused_computation.2 | convolution fusion | flops 2160066560 | bytes 25690112 | tf_op jit(solution)/shard_map/dot_general | solution.py:17
  390.8 8.1 %fusion.1 = bf16[1,512,4096]{1,2,0:T(8,128)(2,1)} fusion(f32[512,4096]{0,1:T(8,128)} %bitcast_add_fusion.1, bf16[1,512,4096]{1,2,0:T(8,128)(2,1)} %copy.21), kind=kLoop, calls=%fused_computation.11 | loop fusion | flops 8388608 | bytes 16777216 | tf_op jit(solution)/shard_map/broadcast_in_dim | solution.py:41
  398.9 6.3 %copy.26 = bf16[1,512,4096]{2,1,0:T(8,128)(2,1)} copy(bf16[1,512,4096]{1,2,0:T(8,128)(2,1)} %fusion) | data formatting | bytes 8388608
  405.2 6.3 %copy.27 = bf16[1,512,4096]{2,1,0:T(8,128)(2,1)} copy(bf16[1,512,4096]{1,2,0:T(8,128)(2,1)} %fusion.1) | data formatting | bytes 8388608
  411.5 8.9 %copy.28 = f32[1,512,4096]{2,1,0:T(8,128)} copy(f32[1,512,4096]{1,2,0:T(8,128)} %bitcast.77) | data formatting | bytes 16777216
  420.4 8.9 %copy.29 = f32[1,512,4096]{2,1,0:T(8,128)} copy(f32[1,512,4096]{1,2,0:T(8,128)} %bitcast.78) | data formatting | bytes 16777216
  (30 shorter events, 12.6 us)
Async XLA Ops:
  7.2 87.1 %reduce-scatter.3.cloned.1.call-start = ((), (), s32[]{:S(2)}) async-start(), calls=%async_computation.2 | async-start | bytes 5242880 | tf_op jit(solution)/shard_map/reduce_scatter | solution.py:68
  16.2 78.1 %copy-start.4 = (bf16[1,128,4096]{2,1,0:T(8,128)(2,1)S(1)}, bf16[1,128,4096]{2,1,0:T(8,128)(2,1)}, u32[]{:S(2)}) copy-start(bf16[1,128,4096]{2,1,0:T(8,128)(2,1)} %param.16) | copy-start | bytes 3145732
  16.2 78.1 %copy-start.5 = (bf16[1,128,4096]{2,1,0:T(8,128)(2,1)S(1)}, bf16[1,128,4096]{2,1,0:T(8,128)(2,1)}, u32[]{:S(2)}) copy-start(bf16[1,128,4096]{2,1,0:T(8,128)(2,1)} %param.15) | copy-start | bytes 3145732
  16.2 161.2 %all-gather.8.cloned.1.call-start = ((), (), s32[]{:S(2)}) async-start(), calls=%async_computation.4 | async-start | bytes 5242880 | tf_op jit(solution)/shard_map/all_gather | solution.py:77
  98.4 160.5 %all-gather.6.cloned.1.call-start = ((), (), s32[]{:S(2)}) async-start(), calls=%async_computation.3 | async-start | bytes 5242880 | tf_op jit(solution)/shard_map/all_gather | solution.py:76
  99.1 241.2 %all-gather.10.cloned.1.call-start = ((), (), s32[]{:S(2)}) async-start(), calls=%async_computation.6 | async-start | bytes 5242880 | tf_op jit(solution)/shard_map/all_gather | solution.py:75
  99.7 288.9 %reduce-scatter.5.cloned.1.call-start = ((), (), s32[]{:S(2)}) async-start(), calls=%async_computation.5 | async-start | bytes 786432 | tf_op jit(solution)/shard_map/reduce_scatter | solution.py:85
  137.2 6.5 %copy-start.6 = (bf16[1,256,512]{2,1,0:T(8,128)(2,1)S(1)}, bf16[1,256,512]{2,1,0:T(8,128)(2,1)}, u32[]{:S(2)}) copy-start(bf16[1,256,512]{2,1,0:T(8,128)(2,1)} %param.13) | copy-start | bytes 786436
  350.1 3.4 copy-start.1
  353.5 5.8 %copy-start.3 = (bf16[1,512,4096]{1,2,0:T(8,128)(2,1)S(1)}, bf16[1,512,4096]{1,2,0:T(8,128)(2,1)}, u32[]{:S(2)}) copy-start(bf16[1,512,4096]{1,2,0:T(8,128)(2,1)} %copy.23) | copy-start | bytes 12582916
  368.1 8.8 %copy-start = (f32[512,4096]{0,1:T(8,128)}, f32[512,4096]{0,1:T(8,128)S(1)}, u32[]{:S(2)}) copy-start(f32[512,4096]{0,1:T(8,128)S(1)} %bitcast_add_fusion.2) | copy-start | bytes 25165828
  368.1 8.7 %copy-start.2 = (bf16[1,512,4096]{1,2,0:T(8,128)(2,1)S(1)}, bf16[1,512,4096]{1,2,0:T(8,128)(2,1)}, u32[]{:S(2)}) copy-start(bf16[1,512,4096]{1,2,0:T(8,128)(2,1)} %copy.25) | copy-start | bytes 12582916
  388.6 40.7 %collective-permute-start = (bf16[256,512]{1,0:T(8,128)(2,1)}, bf16[256,512]{1,0:T(8,128)(2,1)S(1)}, u32[]{:S(2)}, u32[]{:S(2)}) collective-permute-start(bf16[256,512]{1,0:T(8,128)(2,1)} %reduce-scatter.5.cloned.1.call-done), channel_id=1, source_target_pairs={{8,0},{16,8},{24,16},{9,1},{17,9},{25,17},{10,2},{18,10},{26,18},{... | collective-permute-start | bytes 786440 | tf_op jit(solution)/shard_map/ppermute | solution.py:13
Sparse Core Ops, SparseCore 0:
  16.3 77.8 reduce-scatter.2
  98.5 78.8 all-gather.7
  179.6 79.2 all-gather.5
  261.0 79.2 all-gather.9
  342.5 9.1 reduce-scatter.4
where the time goes:
time: 442 us; the launch traced here: 437 us
  waiting for transfers between devices  261 us (59%)
  local copies, waits for them, and re-layouts  78.5 us (18%)
  matrix products  49.2 us (11%)
  other arithmetic  26.7 us (6%)
  between operations  13.8 us (3%)
  blocking collectives  4.74 us (1%)
    unnamed x25, local copies, waits for them, and re-layouts  78.5 us
    reduce_scatter x1, waiting for transfers between devices, shards(): lax.psum_scatter(contract(grad_block, down_local, 1, 1).astype(jnp.bfloat...  78 us
    all_gather x1, waiting for transfers between devices, shards(): gate_piece = lax.all_gather(gate_grad, 'row', axis=0, tiled=True)  75.7 us
    all_gather x1, waiting for transfers between devices, shards(): hidden_piece = lax.all_gather(hidden_saved, 'row', axis=0, tiled=True)  74.7 us
    dot_general x6, matrix products, contract(): lax.dot_general(left, right, (((left_dim,), (right_dim,)), ((), ())), pre...  49.2 us
    all_gather x1, waiting for transfers between devices, shards(): up_piece = lax.all_gather(up_grad, 'row', axis=0, tiled=True)  31.3 us
    broadcast_in_dim x3, other arithmetic, sghmc_step(): return (fresh[None], moved[None])  22.6 us
  transfers between devices with their start and end apart: 6, of which 4 were waited for; matrix products, arithmetic and copies ran while one was open for 32% of the time, Pallas kernels for 0%

commit v1 on v0

v1 whole, which is shorter than its diff:
```python
import functools

import jax
import jax.numpy as jnp
from jax import lax
from jax.experimental import pallas as pl
from jax.experimental.pallas import tpu as pltpu
from jax.sharding import PartitionSpec as P

FRICTION = 0.1
DRIFT = 0.01
CHUNKS = (2, 2, 2, 1, 1)
VMEM_LIMIT = 56 * 1024 * 1024


def from_behind(shard, axis, by):
    size = lax.axis_size(axis)
    pairs = [(i, i + by) for i in range(size) if 0 <= i + by < size]
    return lax.ppermute(shard, axis, pairs)


def contract(left, right, left_dim, right_dim):
    return lax.dot_general(
        left, right, (((left_dim,), (right_dim,)), ((), ())), preferred_element_type=jnp.float32
    )


def moved_and_fresh(weight, momentum, gradient, noise, kick_scale):
    moved = (
        (1.0 - FRICTION) * momentum
        - kick_scale * gradient
        + (2.0 * FRICTION) ** 0.5 * noise.astype(jnp.float32)
    )
    fresh = (weight.astype(jnp.float32) + DRIFT * moved).astype(jnp.bfloat16)
    return moved, fresh


def add_kernel(left, right, *rest):
    total = rest[-1]
    rows = min(128, left.shape[0])

    @pl.loop(0, left.shape[0] // rows)
    def _(step):
        at = pl.ds(pl.multiple_of(step * rows, rows), rows)
        total[at, :] = left[at, :] + right[at, :]


def add_wide(left, right, ties=()):
    return pl.pallas_call(
        add_kernel,
        in_specs=[pl.BlockSpec(memory_space=pltpu.VMEM)] * 2
        + [pl.BlockSpec(memory_space=pl.ANY)] * len(ties),
        out_specs=pl.BlockSpec(memory_space=pltpu.VMEM),
        out_shape=jax.ShapeDtypeStruct(left.shape, jnp.bfloat16),
        cost_estimate=pl.CostEstimate(
            flops=left.size, bytes_accessed=6 * left.size, transcendentals=0
        ),
        name="add_wide",
    )(left, right, *ties)


def same_kernel(*refs):
    del refs


def after(value, *ties):
    anywhere = pl.BlockSpec(memory_space=pl.ANY)
    return pl.pallas_call(
        same_kernel,
        in_specs=[anywhere] * (1 + len(ties)),
        out_specs=anywhere,
        out_shape=jax.ShapeDtypeStruct(value.shape, value.dtype),
        input_output_aliases={0: 0},
        cost_estimate=pl.CostEstimate(flops=0, bytes_accessed=0, transcendentals=0),
        name="after",
    )(value, *ties)


def tile_of(width, largest=512):
    for tile in (largest, 256, 128):
        if width % tile == 0:
            return tile
    return width


def pre_grads(flag, received, held, gate_factor, up_factor):
    hidden_grad = jnp.where(
        flag[0] == 1, received[...].astype(jnp.float32), held[...].astype(jnp.float32)
    )
    gate_grad = (hidden_grad * gate_factor[...].astype(jnp.float32)).astype(jnp.bfloat16)
    up_grad = (hidden_grad * up_factor[...].astype(jnp.float32)).astype(jnp.bfloat16)
    return gate_grad, up_grad


def update_kernel(
    kick_scale,
    with_part,
    first,
    flag,
    received,
    held,
    gate_factor,
    up_factor,
    inputs_t,
    gate_weight,
    up_weight,
    momentum_gate,
    momentum_up,
    noise_gate,
    noise_up,
    *rest,
):
    if with_part:
        part = rest[-1]
        rest = rest[:-1]

        @pl.when(pl.program_id(0) == 0)
        def _():
            part[...] = jnp.zeros_like(part) if first else rest[0][...]

    new_gate, new_up, next_gate, next_up = rest[-4:]
    gate_grad, up_grad = pre_grads(flag, received, held, gate_factor, up_factor)
    gate_here = gate_weight[...]
    up_here = up_weight[...]
    if with_part:
        part[...] += contract(gate_grad, gate_here, 1, 1) + contract(up_grad, up_here, 1, 1)
    gate_wgrad = contract(inputs_t[...], gate_grad, 1, 0)
    moved, fresh = moved_and_fresh(
        gate_here, momentum_gate[...], gate_wgrad, noise_gate[...], kick_scale
    )
    next_gate[...] = moved
    new_gate[...] = fresh
    up_wgrad = contract(inputs_t[...], up_grad, 1, 0)
    moved, fresh = moved_and_fresh(up_here, momentum_up[...], up_wgrad, noise_up[...], kick_scale)
    next_up[...] = moved
    new_up[...] = fresh


def chunk_specs(start, tokens, rows, width, tile):
    steps = width // tile
    at = start // tile
    here = pl.BlockSpec((tokens, tile), lambda j: (0, j))
    there = pl.BlockSpec((tokens, tile), lambda j: (0, at + j))
    block = pl.BlockSpec((rows, tile), lambda j: (0, at + j))
    flag = pl.BlockSpec(memory_space=pltpu.SMEM)
    return steps, block, [flag, here, here, there, there]


def part_kernel(
    halves, col, flag, received, held, gate_factor, up_factor, gate_weight, up_weight, before, *rest
):
    outs, part = rest[:-1], rest[-1]

    @pl.when(pl.program_id(0) == 0)
    def _():
        part[...] = before[...]

    gate_grad, up_grad = pre_grads(flag, received, held, gate_factor, up_factor)
    part[...] += contract(gate_grad, gate_weight[...], 1, 1) + contract(
        up_grad, up_weight[...], 1, 1
    )

    @pl.when(pl.program_id(0) == pl.num_programs(0) - 1)
    def _():
        if not halves:
            outs[0][...] = part[...].astype(jnp.bfloat16)
            return
        half = part.shape[0] // 2
        for out, which in ((outs[0], col[0]), (outs[1], 1 - col[0])):
            at = pl.ds(pl.multiple_of(which * half, half), half)
            out[...] = part[at, :].astype(jnp.bfloat16)


def part_step(start, hidden, factors, weights, part, axis):
    received, held, flag = hidden
    tokens, width = held.shape
    rows = weights[0].shape[0]
    halves = lax.axis_size(axis) == 2
    tile = tile_of(width)
    steps, block, in_specs = chunk_specs(start, tokens, rows, width, tile)
    whole = pl.BlockSpec((tokens, rows), lambda j: (0, 0))
    half = pl.BlockSpec((tokens // 2, rows), lambda j: (0, 0))
    index = lax.axis_index(axis).astype(jnp.int32).reshape((1,))
    return pl.pallas_call(
        functools.partial(part_kernel, halves),
        grid=(steps,),
        in_specs=[pl.BlockSpec(memory_space=pltpu.SMEM)] + in_specs + [block] * 2 + [whole],
        out_specs=[half] * 2 if halves else [whole],
        out_shape=[jax.ShapeDtypeStruct((tokens // 2, rows), jnp.bfloat16)] * 2
        if halves
        else [jax.ShapeDtypeStruct((tokens, rows), jnp.bfloat16)],
        scratch_shapes=[pltpu.VMEM((tokens, rows), jnp.float32)],
        compiler_params=pltpu.CompilerParams(vmem_limit_bytes=VMEM_LIMIT),
        cost_estimate=pl.CostEstimate(
            flops=4 * tokens * rows * width,
            bytes_accessed=(8 * tokens + 4 * rows) * width + 6 * tokens * rows,
            transcendentals=0,
        ),
        name="part_step",
    )(index, flag, received, held, *factors, *weights, part)


def update_step(kick_scale, start, hidden, factors, inputs_t, arrays, part, made, with_part):
    received, held, flag = hidden
    tokens, width = held.shape
    rows, columns = arrays[0].shape
    tile = tile_of(width, 512 if with_part else 256)
    first = part is None
    steps, block, in_specs = chunk_specs(start, tokens, rows, width, tile)
    whole_inputs = pl.BlockSpec((rows, tokens), lambda j: (0, 0))
    whole_part = pl.BlockSpec((tokens, rows), lambda j: (0, 0))
    in_specs += [whole_inputs] + [block] * 6
    operands = [flag, received, held, *factors, inputs_t, *arrays]
    if with_part and not first:
        in_specs.append(whole_part)
        operands.append(part)
    aliases = {}
    if made is not None:
        aliases = {len(operands) + i: i for i in range(4)}
        in_specs += [pl.BlockSpec(memory_space=pl.ANY)] * 4
        operands += made
    shape = (rows, columns)
    out_specs = [block] * 4
    out_shape = [
        jax.ShapeDtypeStruct(shape, jnp.bfloat16),
        jax.ShapeDtypeStruct(shape, jnp.bfloat16),
        jax.ShapeDtypeStruct(shape, jnp.float32),
        jax.ShapeDtypeStruct(shape, jnp.float32),
    ]
    if with_part:
        out_specs.append(whole_part)
        out_shape.append(jax.ShapeDtypeStruct((tokens, rows), jnp.float32))
    outs = pl.pallas_call(
        functools.partial(update_kernel, kick_scale, with_part, first),
        grid=(steps,),
        in_specs=in_specs,
        out_specs=out_specs,
        out_shape=out_shape,
        input_output_aliases=aliases,
        compiler_params=pltpu.CompilerParams(vmem_limit_bytes=VMEM_LIMIT),
        cost_estimate=pl.CostEstimate(
            flops=(8 if with_part else 4) * tokens * rows * width,
            bytes_accessed=(8 * tokens + 28 * rows) * width,
            transcendentals=0,
        ),
        name="update_step",
    )(*operands)
    return (outs[4] if with_part else None), tuple(outs[:4])


def saved_kernel(kick_scale, size, table, *refs):
    gate_pieces = refs[: 2 * size - 1]
    up_pieces = refs[2 * size - 1 : 4 * size - 2]
    grads, weight, momentum, noise = refs[4 * size - 2 : 4 * size + 2]
    new_down, next_down, gate_factor, up_factor, hidden = refs[4 * size + 2 :]
    rows = gate_pieces[0].shape[0]

    def piece(pieces, at):
        if at == 0:
            return pieces[0][...].astype(jnp.float32)
        one, other = pieces[2 * at - 1], pieces[2 * at]
        return jnp.where(
            table[at] == 1, one[...].astype(jnp.float32), other[...].astype(jnp.float32)
        )

    for part in range(size):
        gate_wide = piece(gate_pieces, part)
        up_wide = piece(up_pieces, part)
        sigmoid_gate = 0.5 + 0.5 * jnp.tanh(0.5 * gate_wide)
        silu_gate = gate_wide * sigmoid_gate
        slope = sigmoid_gate * (1.0 + gate_wide * (1.0 - sigmoid_gate))
        at = pl.ds(pl.multiple_of(table[size + part] * rows, rows), rows)
        gate_factor[at, :] = (up_wide * slope).astype(jnp.bfloat16)
        up_factor[at, :] = silu_gate.astype(jnp.bfloat16)
        hidden[at, :] = (silu_gate * up_wide).astype(jnp.bfloat16)
    wgrad = contract(hidden[...], grads[...], 0, 0)
    moved, fresh = moved_and_fresh(weight[...], momentum[...], wgrad, noise[...], kick_scale)
    next_down[...] = moved
    new_down[...] = fresh


def saved_step(kick_scale, size, table, gate_pieces, up_pieces, grads, weight, momentum, noise):
    rows, width = gate_pieces[0][0].shape
    tokens, columns = grads.shape
    tile = tile_of(width)
    pieces = [*gate_pieces, *up_pieces]
    piece_specs = [pl.BlockSpec((rows, tile), lambda j, at=at: (at, j)) for _, at in pieces]
    block = pl.BlockSpec((tile, columns), lambda j: (j, 0))
    whole = pl.BlockSpec((tokens, columns), lambda j: (0, 0))
    factor = pl.BlockSpec((tokens, tile), lambda j: (0, j))
    return pl.pallas_call(
        functools.partial(saved_kernel, kick_scale, size),
        grid=(width // tile,),
        in_specs=[pl.BlockSpec(memory_space=pltpu.SMEM)]
        + piece_specs
        + [whole]
        + [block] * 3,
        out_specs=[block, block, factor, factor],
        out_shape=[
            jax.ShapeDtypeStruct(weight.shape, jnp.bfloat16),
            jax.ShapeDtypeStruct(weight.shape, jnp.float32),
            jax.ShapeDtypeStruct((tokens, width), jnp.bfloat16),
            jax.ShapeDtypeStruct((tokens, width), jnp.bfloat16),
        ],
        scratch_shapes=[pltpu.VMEM((tokens, tile), jnp.bfloat16)],
        compiler_params=pltpu.CompilerParams(vmem_limit_bytes=VMEM_LIMIT),
        cost_estimate=pl.CostEstimate(
            flops=2 * tokens * width * columns,
            bytes_accessed=12 * tokens * width + 14 * width * columns,
            transcendentals=tokens * width,
        ),
        name="saved_step",
    )(table, *[array for array, _ in pieces], grads, weight, momentum, noise)


def relay_step(behind, ahead, axis, step):
    size = lax.axis_size(axis)
    up = [(i, i + 1) for i in range(step - 1, size - 1)]
    down = [(i, i - 1) for i in range(1, size - step + 1)]
    return lax.ppermute(behind, axis, up), lax.ppermute(ahead, axis, down)


def relayed(arrays, axis):
    size = lax.axis_size(axis)
    me = lax.axis_index(axis).astype(jnp.int32)
    pieces = []
    for own in arrays:
        behind, ahead = [own], [own]
        for step in range(1, size):
            from_back, from_front = relay_step(behind[-1], ahead[-1], axis, step)
            behind.append(from_back)
            ahead.append(from_front)
        pieces.append([(own, 0)])
        for back in range(1, size):
            pieces[-1] += [(behind[back], 0), (ahead[size - back], 0)]
    backs = jnp.arange(size, dtype=jnp.int32)
    table = jnp.concatenate([(me >= backs).astype(jnp.int32), (me - backs + size) % size])
    return pieces, table


OUTWARD = ((1, 0), (2, 3))
INWARD = ((0, 1), (3, 2))
MIDDLE = ((1, 2), (2, 1))


def relayed_by_four(arrays, terms, axis):
    me = lax.axis_index(axis).astype(jnp.int32)
    gate, up = arrays
    gate_b1, gate_a1 = relay_step(gate, gate, axis, 1)
    up_b1, up_a1 = relay_step(up, up, axis, 1)
    gate_b2, gate_a2 = relay_step(gate_b1, gate_a1, axis, 2)
    up_b2, up_a2 = relay_step(up_b1, up_a1, axis, 2)
    gate_out3 = lax.ppermute(jnp.where(me == 1, gate_a2, gate_b2), axis, OUTWARD)
    up_out3 = lax.ppermute(jnp.where(me == 1, up_a2, up_b2), axis, OUTWARD)
    terms, ins = list(terms), []
    for at in range(len(terms)):
        if at in (1, 2):
            terms[at] = after(terms[at], ins[-1])
        ins.append(lax.ppermute(terms[at], axis, INWARD))
    inner, mids = [], []
    sums = []

    def send_inner(at, *ties):
        inner.append(add_wide(terms[at], ins[at], ties))
        mids.append(lax.ppermute(inner[at], axis, MIDDLE))

    def send_total(at, *ties):
        sums.append(outward_sum(add_wide(inner[at], mids[at], ties), axis))

    send_inner(0, up_a2, up_b2)
    send_inner(1, gate_out3)
    send_total(0, gate_out3)
    send_inner(2, mids[0])
    send_total(1, up_out3)
    send_inner(3, mids[1])
    send_inner(4, mids[2])
    pieces = [
        [(gate, 0), (gate_a1, 0), (gate_b1, 0), (gate_a2, 0), (gate_b2, 0)],
        [(up, 0), (up_a1, 0), (up_b1, 0), (up_a2, 0), (up_b2, 0)],
    ]
    pieces[0] += [(gate_out3, 0), (gate_b1, 0)]
    pieces[1] += [(up_out3, 0), (up_b1, 0)]
    end = (me == 0) | (me == 3)
    flags = [me < 3, me < 3, me < 2, end]
    places = [me, jnp.where(me < 3, me + 1, 2), (me + 2) % 4, jnp.where(end, 3 - me, me - 1)]
    table = jnp.stack([flag.astype(jnp.int32) for flag in flags] + places)
    return pieces, table, sums, send_total


def inward_sum(term, axis, ties):
    size = lax.axis_size(axis)
    held = term
    for step in range(size // 2 - 1):
        pairs = [(step, step + 1), (size - 1 - step, size - 2 - step)]
        held = add_wide(held, lax.ppermute(held, axis, pairs), ties if step == 0 else ())
    return held


def middle_sum(held, axis, ties):
    half = lax.axis_size(axis) // 2
    across = lax.ppermute(held, axis, [(half - 1, half), (half, half - 1)])
    return add_wide(held, across, ties), across


def outward_sum(held, axis):
    size = lax.axis_size(axis)
    index = lax.axis_index(axis)
    half = size // 2
    received, flag = held, jnp.zeros((1,), jnp.int32)
    for step in range(half - 1):
        if step:
            held = jnp.where(flag[0] == 1, received, held)
        pairs = [(half - 1 - step, half - 2 - step), (half + step, half + 1 + step)]
        received = lax.ppermute(held, axis, pairs)
        arrived = (index == half - 2 - step) | (index == half + 1 + step)
        flag = arrived.astype(jnp.int32).reshape((1,))
    return received, held, flag


def row_sums(terms, axis):
    sums = []
    for term in terms:
        if lax.axis_size(axis) % 2:
            total = lax.psum(term, axis)
            sums.append((total, total, jnp.zeros((1,), jnp.int32)))
        else:
            held, _ = middle_sum(inward_sum(term, axis, ()), axis, ())
            sums.append(outward_sum(held, axis))
    return sums


def parts_sum(parts, axis):
    if len(parts) == 1:
        return lax.psum_scatter(parts[0], axis, scatter_dimension=0, tiled=True)
    return add_wide(parts[0], lax.ppermute(parts[1], axis, [(0, 1), (1, 0)]))


def shards(
    section_inputs,
    out_grad,
    saved_gate,
    saved_up,
    gate_weight,
    up_weight,
    down_weight,
    momentum_gate,
    momentum_up,
    momentum_down,
    noise_gate,
    noise_up,
    noise_down,
):
    size = lax.axis_size("row")
    saved = (saved_gate[0], saved_up[0])
    grads_full = lax.all_gather(out_grad[0], "col", axis=0, tiled=True)
    inputs_full = lax.all_gather(section_inputs[0], "col", axis=0, tiled=True)
    inputs_t = inputs_full.T
    tokens = inputs_full.shape[0]
    kick_scale = float(tokens) ** (-0.5)
    down_local = down_weight[0]
    unit = down_local.shape[0] // sum(CHUNKS)
    starts = [unit * sum(CHUNKS[:at]) for at in range(len(CHUNKS))]
    stops = starts[1:] + [down_local.shape[0]]
    terms = [
        contract(grads_full, down_local[start:stop], 1, 1).astype(jnp.bfloat16)
        for start, stop in zip(starts, stops)
    ]
    send_total = None
    if size == 4:
        pieces, table, sums, send_total = relayed_by_four(saved, terms, "row")
    else:
        pieces, table = relayed(saved, "row")
        sums = row_sums(terms, "row")

    new_down, next_down, *factors = saved_step(
        kick_scale,
        size,
        table,
        *pieces,
        grads_full,
        down_local,
        momentum_down[0],
        noise_down[0],
    )
    weights = (gate_weight[0], up_weight[0])
    arrays = weights + (momentum_gate[0], momentum_up[0], noise_gate[0], noise_up[0])
    if send_total is not None:
        send_total(2, factors[0])
    part, made = None, None
    for at, start in enumerate(starts[:-1]):
        part, made = update_step(
            kick_scale, start, sums[at], factors, inputs_t, arrays, part, made, True
        )
        if at < 2 and send_total is not None:
            send_total(3 + at, part)
    parts = part_step(starts[-1], sums[-1], factors, weights, part, "col")
    _, made = update_step(
        kick_scale, starts[-1], sums[-1], factors, inputs_t, arrays, None, made, False
    )
    new_gate, new_up, next_gate, next_up = made
    input_grad = parts_sum(parts, "col")
    passed = from_behind(input_grad, "section", -1)
    return tuple(
        value[None]
        for value in (passed, new_gate, new_up, new_down, next_gate, next_up, next_down)
    )


def solution(mesh):
    in_specs = (
        P("section", "col", "row"),
        P("section", "col", "row"),
        P("section", "row", "col"),
        P("section", "row", "col"),
        P("section", "row", "col"),
        P("section", "row", "col"),
        P("section", "col", "row"),
        P("section", "row", "col"),
        P("section", "row", "col"),
        P("section", "col", "row"),
        P("section", "row", "col"),
        P("section", "row", "col"),
        P("section", "col", "row"),
    )
    out_specs = (
        P("section", "col", "row"),
        P("section", "row", "col"),
        P("section", "row", "col"),
        P("section", "col", "row"),
        P("section", "row", "col"),
        P("section", "row", "col"),
        P("section", "col", "row"),
    )
    return jax.shard_map(shards, mesh=mesh, in_specs=in_specs, out_specs=out_specs, check_vma=False)
```

time: 442 us -> 276 us (0.62)
  waiting for transfers between devices: 261 us -> 85.6 us
  Pallas kernels: 0 us -> 91.5 us
  local copies, waits for them, and re-layouts: 78.5 us -> 11.5 us
  starting transfers between devices: 2.45 us -> 61.2 us
  matrix products: 49.2 us -> 14.1 us
  other arithmetic: 26.7 us -> 4.66 us
  between operations: 13.8 us -> 1.08 us
    all_gather x3 -> x0, waiting for transfers between devices: 182 us -> none  [the longest x1 75.7 us: shards(): gate_piece = lax.all_gather(gate_grad, 'row', axis=0, tiled=True)]
    pallas_call x0 -> x20, Pallas kernels: none -> 91.5 us  [the longest x5 38.7 us: update_step(): pl.pallas_call(functools.partial(update_kernel, kick_scale, with_part, fi...]
    ppermute x0 -> x26, waiting for transfers between devices: none -> 81.7 us  [the longest x8 33.4 us: relay_step(): return (lax.ppermute(behind, axis, up), lax.ppermute(ahead, axis, down))]
    reduce_scatter x2 -> x0, waiting for transfers between devices: 78 us -> none  [the longest x1 78 us: shards(): lax.psum_scatter(contract(grad_block, down_local, 1, 1).astype(jnp.bfloat...]
    unnamed x25 -> x34, local copies, waits for them, and re-layouts: 78.5 us -> 10.9 us
    ppermute x0 -> x26, starting transfers between devices: none -> 58.8 us  [the longest x8 22.4 us: relay_step(): return (lax.ppermute(behind, axis, up), lax.ppermute(ahead, axis, down))]
    dot_general x6 -> x5, matrix products: 49.2 us -> 14.1 us  [contract(): lax.dot_general(left, right, (((left_dim,), (right_dim,)), ((), ())), pre...]
    broadcast_in_dim x3 -> x0, other arithmetic: 22.6 us -> none  [sghmc_step(): return (fresh[None], moved[None])]
  transfers between devices with their start and end apart: 6 -> 27, of which waited for: 4 -> 10; matrix products, arithmetic and copies ran while one was open for 32% -> 7% of each run, Pallas kernels for 0% -> 31%
where the time goes in v1:
time: 276 us; the launch traced here: 274 us
  Pallas kernels  91.5 us (33%)
  waiting for transfers between devices  85.6 us (31%)
  starting transfers between devices  61.2 us (22%)
  matrix products  14.1 us (5%)
  local copies, waits for them, and re-layouts  11.5 us (4%)
  blocking collectives  4.71 us (2%)
  other arithmetic  4.66 us (2%)
    pallas_call x5, Pallas kernels, update_step(): pl.pallas_call(functools.partial(update_kernel, kick_scale, with_part, fi...  38.7 us
    ppermute x8, waiting for transfers between devices, relay_step(): return (lax.ppermute(behind, axis, up), lax.ppermute(ahead, axis, down))  33.4 us
    pallas_call x11, Pallas kernels, add_wide(): pl.pallas_call(add_kernel, in_specs=[pl.BlockSpec(memory_space=pltpu.VMEM...  25.9 us
    ppermute x5, waiting for transfers between devices, relayed_by_four(): ins.append(lax.ppermute(terms[at], axis, INWARD))  24.4 us
    pallas_call x1, Pallas kernels, saved_step(): pl.pallas_call(functools.partial(saved_kernel, kick_scale, size), grid=(w...  23.2 us
    ppermute x8, starting transfers between devices, relay_step(): return (lax.ppermute(behind, axis, up), lax.ppermute(ahead, axis, down))  22.4 us
    dot_general x5, matrix products, contract(): lax.dot_general(left, right, (((left_dim,), (right_dim,)), ((), ())), pre...  14.1 us
    ppermute x5, starting transfers between devices, send_inner(): mids.append(lax.ppermute(inner[at], axis, MIDDLE))  13.9 us
  transfers between devices with their start and end apart: 27, of which 10 were waited for; matrix products, arithmetic and copies ran while one was open for 7% of the time, Pallas kernels for 31%

profile of v1, /device:TPU:10, one launch (start us, length us, event | category | flops | bytes accessed | tf_op | source)
XLA Modules:
  0.0 274.4 jit_solution(17736605889571903557)
XLA Ops:
  0.6 3.5 %collective-permute-start.13 = (bf16[128,4096]{1,0:T(8,128)(2,1)}, bf16[128,4096]{1,0:T(8,128)(2,1)S(1)}, u32[]{:S(2)}, u32[]{:S(2)}) collective-permute-start(bf16[128,4096]{1,0:T(8,128)(2,1)} %bitcast.103), channel_id=1, source_target_pairs={{0,2},{2,4},{4,6},{1,3},{3,5},{5,7},{8,10},{10,12},{12,14},{9,11},... | collective-permute-start | bytes 3145736 | tf_op jit(solution)/shard_map/ppermute | solution.py:320
  9.0 3.1 %convolution_convert_fusion.left = bf16[512,1024]{1,0:T(8,128)(2,1)} fusion(bf16[1,4096,512]{2,1,0:T(8,128)(2,1)} %param.19, bf16[1,512,512]{2,1,0:T(8,128)(2,1)S(1)} %all-gather), kind=kOutput, calls=%fused_computation | convolution fusion | flops 537395200 | bytes 2621440 | tf_op jit(solution)/shard_map/dot_general | solution.py:23
  13.4 3.4 %collective-permute-start.6 = (bf16[128,4096]{1,0:T(8,128)(2,1)}, bf16[128,4096]{1,0:T(8,128)(2,1)}, u32[]{:S(2)}, u32[]{:S(2)}) collective-permute-start(bf16[128,4096]{1,0:T(8,128)(2,1)} %bitcast.100), channel_id=1, source_target_pairs={{0,2},{2,4},{4,6},{1,3},{3,5},{5,7},{8,10},{10,12},{12,14},{9,11},... | collective-permute-start | bytes 3145736 | tf_op jit(solution)/shard_map/ppermute | solution.py:320
  16.8 3.4 %collective-permute-start.4 = (bf16[128,4096]{1,0:T(8,128)(2,1)}, bf16[128,4096]{1,0:T(8,128)(2,1)}, u32[]{:S(2)}, u32[]{:S(2)}) collective-permute-start(bf16[128,4096]{1,0:T(8,128)(2,1)} %bitcast.101), channel_id=1, source_target_pairs={{2,0},{4,2},{6,4},{3,1},{5,3},{7,5},{10,8},{12,10},{14,12},{11,9},... | collective-permute-start | bytes 3145736 | tf_op jit(solution)/shard_map/ppermute | solution.py:320
  20.3 8.5 %collective-permute-done.13.refs_2_.refs_6_ = bf16[128,4096]{1,0:T(8,128)(2,1)S(1)} collective-permute-done((bf16[128,4096]{1,0:T(8,128)(2,1)}, bf16[128,4096]{1,0:T(8,128)(2,1)S(1)}, u32[]{:S(2)}, u32[]{:S(2)}) %collective-permute-start.13) | collective-permute-done | bytes 1048608 | tf_op jit(solution)/shard_map/ppermute | solution.py:320
  28.8 4.5 %collective-permute-start.14 = (bf16[128,4096]{1,0:T(8,128)(2,1)S(1)}, bf16[128,4096]{1,0:T(8,128)(2,1)}, u32[]{:S(2)}, u32[]{:S(2)}) collective-permute-start(bf16[128,4096]{1,0:T(8,128)(2,1)S(1)} %collective-permute-done.13.refs_2_.refs_6_), channel_id=1, source_target_pairs={{2,4},{4,6},{3,5},{5,7},{10,12},{12,14},{11,13},{13,15},{18,20},{2... | collective-permute-start | bytes 3145736 | tf_op jit(solution)/shard_map/ppermute | solution.py:320
  38.1 13.1 %collective-permute-done.1.refs_1_.right = bf16[512,1024]{1,0:T(8,128)(2,1)S(1)} collective-permute-done((bf16[512,1024]{1,0:T(8,128)(2,1)}, bf16[512,1024]{1,0:T(8,128)(2,1)S(1)}, u32[]{:S(2)}, u32[]{:S(2)}) %collective-permute-start.1) | collective-permute-done | bytes 1048608 | tf_op jit(solution)/shard_map/ppermute | solution.py:359
  53.5 20.3 %collective-permute-done.6.refs_9_.refs_13_ = bf16[128,4096]{1,0:T(8,128)(2,1)} collective-permute-done((bf16[128,4096]{1,0:T(8,128)(2,1)}, bf16[128,4096]{1,0:T(8,128)(2,1)}, u32[]{:S(2)}, u32[]{:S(2)}) %collective-permute-start.6) | collective-permute-done | bytes 1048608 | tf_op jit(solution)/shard_map/ppermute | solution.py:320
  83.9 11.2 %collective-permute-done.2.refs_1_.right = bf16[512,1024]{1,0:T(8,128)(2,1)} collective-permute-done((bf16[512,1024]{1,0:T(8,128)(2,1)}, bf16[512,1024]{1,0:T(8,128)(2,1)}, u32[]{:S(2)}, u32[]{:S(2)}) %collective-permute-start.2) | collective-permute-done | bytes 1048608 | tf_op jit(solution)/shard_map/ppermute | solution.py:359
  96.5 4.6 %collective-permute-done.5.rest_0_.refs_10_ = bf16[128,4096]{1,0:T(8,128)(2,1)S(1)} collective-permute-done((bf16[128,4096]{1,0:T(8,128)(2,1)}, bf16[128,4096]{1,0:T(8,128)(2,1)S(1)}, u32[]{:S(2)}, u32[]{:S(2)}) %collective-permute-start.5) | collective-permute-done | bytes 1048608 | tf_op jit(solution)/shard_map/ppermute | solution.py:320
  104.6 3.1 %collective-permute-start.8 = (bf16[512,1024]{1,0:T(8,128)(2,1)}, bf16[512,1024]{1,0:T(8,128)(2,1)S(1)}, u32[]{:S(2)}, u32[]{:S(2)}) collective-permute-start(bf16[512,1024]{1,0:T(8,128)(2,1)} %add_wide.11.left), channel_id=1, source_target_pairs={{2,4},{4,2},{3,5},{5,3},{10,12},{12,10},{11,13},{13,11},{18,20},{2... | collective-permute-start | bytes 3145736 | tf_op jit(solution)/shard_map/ppermute | solution.py:365
  112.0 11.5 %collective-permute-done.15.rest_0_.refs_5_ = bf16[128,4096]{1,0:T(8,128)(2,1)S(1)} collective-permute-done((bf16[128,4096]{1,0:T(8,128)(2,1)}, bf16[128,4096]{1,0:T(8,128)(2,1)S(1)}, u32[]{:S(2)}, u32[]{:S(2)}) %collective-permute-start.15) | collective-permute-done | bytes 1048608 | tf_op jit(solution)/shard_map/ppermute | solution.py:353
  129.0 3.8 %collective-permute-done.8.rest_0_.right = bf16[512,1024]{1,0:T(8,128)(2,1)S(1)} collective-permute-done((bf16[512,1024]{1,0:T(8,128)(2,1)}, bf16[512,1024]{1,0:T(8,128)(2,1)S(1)}, u32[]{:S(2)}, u32[]{:S(2)}) %collective-permute-start.8) | collective-permute-done | bytes 1048608 | tf_op jit(solution)/shard_map/ppermute | solution.py:365
  136.4 3.1 %collective-permute-start.9 = (bf16[512,1024]{1,0:T(8,128)(2,1)}, bf16[512,1024]{1,0:T(8,128)(2,1)S(1)}, u32[]{:S(2)}, u32[]{:S(2)}) collective-permute-start(bf16[512,1024]{1,0:T(8,128)(2,1)} %add_wide.12.left), channel_id=1, source_target_pairs={{2,4},{4,2},{3,5},{5,3},{10,12},{12,10},{11,13},{13,11},{18,20},{2... | collective-permute-start | bytes 3145736 | tf_op jit(solution)/shard_map/ppermute | solution.py:365
  148.2 7.1 %collective-permute-done.16.right.rest_0_ = bf16[512,1024]{1,0:T(8,128)(2,1)S(1)} collective-permute-done((bf16[512,1024]{1,0:T(8,128)(2,1)}, bf16[512,1024]{1,0:T(8,128)(2,1)S(1)}, u32[]{:S(2)}, u32[]{:S(2)}) %collective-permute-start.16) | collective-permute-done | bytes 1048608 | tf_op jit(solution)/shard_map/ppermute | solution.py:365
  164.6 23.2 %saved_step.1 = (bf16[4096,512]{1,0:T(8,128)(2,1)}, f32[4096,512]{1,0:T(8,128)}, bf16[512,4096]{1,0:T(8,128)(2,1)}, bf16[512,4096]{1,0:T(8,128)(2,1)}) custom-call(s32[8]{0:T(128)} %stack.37.table, bf16[128,4096]{1,0:T(8,128)(2,1)} %bitcast.105, bf16[128,4096]{1,0:T(8,128)(2,1)} %collective-permute-done.11.refs_1_, bf16[128,4096]{1,0:T(8,128)(2,1)} %copy-done.3, ...), custom_call_target="tpu_custom_call" | custom-call | flops 2147483648 | bytes 54525952 | tf_op jit(solution)/shard_map/saved_step/pallas_call | solution.py:291
  191.5 5.4 %collective-permute-start.24 = (bf16[512,1024]{1,0:T(8,128)(2,1)}, bf16[512,1024]{1,0:T(8,128)(2,1)S(1)}, u32[]{:S(2)}, u32[]{:S(2)}) collective-permute-start(bf16[512,1024]{1,0:T(8,128)(2,1)} %add_wide.20.held), channel_id=1, source_target_pairs={{2,0},{4,6},{3,1},{5,7},{10,8},{12,14},{11,9},{13,15},{18,16},{20,... | collective-permute-start | bytes 3145736 | tf_op jit(solution)/shard_map/ppermute | solution.py:414
  209.4 8.8 %update_step.5 = (bf16[512,4096]{1,0:T(8,128)(2,1)}, bf16[512,4096]{1,0:T(8,128)(2,1)}, f32[512,4096]{1,0:T(8,128)}, f32[512,4096]{1,0:T(8,128)}, f32[512,512]{1,0:T(8,128)}) custom-call(s32[1]{0:T(128)} %bitcast.1.flag, bf16[512,1024]{1,0:T(8,128)(2,1)} %collective-permute-done.19.received, bf16[512,1024]{1,0:T(8,128)(2,1)} %add_wide.16.held, ...), custom_call_target="tpu_custom_call" | custom-call | flops 2147483648 | bytes 18874368 | tf_op jit(solution)/shard_map/update_step/pallas_call | solution.py:233
  223.4 9.0 %update_step.6 = (bf16[512,4096]{1,0:T(8,128)(2,1)}, bf16[512,4096]{1,0:T(8,128)(2,1)}, f32[512,4096]{1,0:T(8,128)}, f32[512,4096]{1,0:T(8,128)}, f32[512,512]{1,0:T(8,128)}) custom-call(s32[1]{0:T(128)} %bitcast.1.flag, bf16[512,1024]{1,0:T(8,128)(2,1)} %copy-done.11, ...), custom_call_target="tpu_custom_call", output_to_operand_aliasing={{0}: (13, {}), {1}: (14, {}), {2}: (15, {}), {3}: (16, {})} | custom-call | flops 2147483648 | bytes 18874368 | tf_op jit(solution)/shard_map/update_step/pallas_call | solution.py:233
  237.8 9.0 %update_step.7 = (bf16[512,4096]{1,0:T(8,128)(2,1)}, bf16[512,4096]{1,0:T(8,128)(2,1)}, f32[512,4096]{1,0:T(8,128)}, f32[512,4096]{1,0:T(8,128)}, f32[512,512]{1,0:T(8,128)}) custom-call(s32[1]{0:T(128)} %bitcast.1.flag, bf16[512,1024]{1,0:T(8,128)(2,1)} %copy-done.12, ...), custom_call_target="tpu_custom_call", output_to_operand_aliasing={{0}: (13, {}), {1}: (14, {}), {2}: (15, {}), {3}: (16, {})} | custom-call | flops 2147483648 | bytes 18874368 | tf_op jit(solution)/shard_map/update_step/pallas_call | solution.py:233
  246.8 6.7 %update_step.8 = (bf16[512,4096]{1,0:T(8,128)(2,1)}, bf16[512,4096]{1,0:T(8,128)(2,1)}, f32[512,4096]{1,0:T(8,128)}, f32[512,4096]{1,0:T(8,128)}, f32[512,512]{1,0:T(8,128)}) custom-call(s32[1]{0:T(128)} %bitcast.1.flag, ...), custom_call_target="tpu_custom_call", output_to_operand_aliasing={{0}: (13, {}), {1}: (14, {}), {2}: (15, {}), {3}: (16, {})} | custom-call | flops 1073741824 | bytes 9437184 | tf_op jit(solution)/shard_map/update_step/pallas_call | solution.py:233
  254.4 3.8 %part_step.1 = (bf16[256,512]{1,0:T(8,128)(2,1)}, bf16[256,512]{1,0:T(8,128)(2,1)}) custom-call(s32[1]{0:T(128)} %bitcast.col, s32[1]{0:T(128)} %bitcast.1.flag, bf16[512,512]{1,0:T(8,128)(2,1)} %copy-done.9, bf16[512,512]{1,0:T(8,128)(2,1)} %add_wide.17.held, bf16[512,4096]{1,0:T(8,128)(2,1)} %get-tuple-element.37.gate_factor.rest_0_, ...), custom_call_target="tpu_custom_call" | custom-call | flops 536870912 | bytes 4718592 | tf_op jit(solution)/shard_map/part_step/pallas_call | solution.py:184
  264.8 5.1 %update_step.9 = (bf16[512,4096]{1,0:T(8,128)(2,1)}, bf16[512,4096]{1,0:T(8,128)(2,1)}, f32[512,4096]{1,0:T(8,128)}, f32[512,4096]{1,0:T(8,128)}) custom-call(s32[1]{0:T(128)} %bitcast.1.flag, bf16[512,512]{1,0:T(8,128)(2,1)} %copy-done.9, ...), custom_call_target="tpu_custom_call", output_to_operand_aliasing={{0}: (12, {}), {1}: (13, {}), {2}: (14, {}), {3}: (15, {})} | custom-call | flops 536870912 | bytes 9437184 | tf_op jit(solution)/shard_map/update_step/pallas_call | solution.py:233
  269.9 3.8 %collective-permute-done.26 = bf16[256,512]{1,0:T(8,128)(2,1)S(1)} collective-permute-done((bf16[256,512]{1,0:T(8,128)(2,1)}, bf16[256,512]{1,0:T(8,128)(2,1)S(1)}, u32[]{:S(2)}, u32[]{:S(2)}) %collective-permute-start.26) | collective-permute-done | bytes 262176 | tf_op jit(solution)/shard_map/ppermute | solution.py:19
  (94 shorter events, 94.3 us)
Async XLA Ops:
  0.6 28.2 %collective-permute-start.13 = (bf16[128,4096]{1,0:T(8,128)(2,1)}, bf16[128,4096]{1,0:T(8,128)(2,1)S(1)}, u32[]{:S(2)}, u32[]{:S(2)}) collective-permute-start(bf16[128,4096]{1,0:T(8,128)(2,1)} %bitcast.103), channel_id=1, source_target_pairs={{0,2},{2,4},{4,6},{1,3},{3,5},{5,7},{8,10},{10,12},{12,14},{9,11},... | collective-permute-start | bytes 3145736 | tf_op jit(solution)/shard_map/ppermute | solution.py:320
  4.1 29.1 %collective-permute-start.11 = (bf16[128,4096]{1,0:T(8,128)(2,1)}, bf16[128,4096]{1,0:T(8,128)(2,1)}, u32[]{:S(2)}, u32[]{:S(2)}) collective-permute-start(bf16[128,4096]{1,0:T(8,128)(2,1)} %bitcast.104), channel_id=1, source_target_pairs={{2,0},{4,2},{6,4},{3,1},{5,3},{7,5},{10,8},{12,10},{14,12},{11,9},... | collective-permute-start | bytes 3145736 | tf_op jit(solution)/shard_map/ppermute | solution.py:320
  12.1 39.2 %collective-permute-start.1 = (bf16[512,1024]{1,0:T(8,128)(2,1)}, bf16[512,1024]{1,0:T(8,128)(2,1)S(1)}, u32[]{:S(2)}, u32[]{:S(2)}) collective-permute-start(bf16[512,1024]{1,0:T(8,128)(2,1)} %convolution_convert_fusion.left), channel_id=1, source_target_pairs={{0,2},{6,4},{1,3},{7,5},{8,10},{14,12},{9,11},{15,13},{16,18},{22,... | collective-permute-start | bytes 3145736 | tf_op jit(solution)/shard_map/ppermute | solution.py:359
  13.4 60.5 %collective-permute-start.6 = (bf16[128,4096]{1,0:T(8,128)(2,1)}, bf16[128,4096]{1,0:T(8,128)(2,1)}, u32[]{:S(2)}, u32[]{:S(2)}) collective-permute-start(bf16[128,4096]{1,0:T(8,128)(2,1)} %bitcast.100), channel_id=1, source_target_pairs={{0,2},{2,4},{4,6},{1,3},{3,5},{5,7},{8,10},{10,12},{12,14},{9,11},... | collective-permute-start | bytes 3145736 | tf_op jit(solution)/shard_map/ppermute | solution.py:320
  16.8 58.4 %collective-permute-start.4 = (bf16[128,4096]{1,0:T(8,128)(2,1)}, bf16[128,4096]{1,0:T(8,128)(2,1)}, u32[]{:S(2)}, u32[]{:S(2)}) collective-permute-start(bf16[128,4096]{1,0:T(8,128)(2,1)} %bitcast.101), channel_id=1, source_target_pairs={{2,0},{4,2},{6,4},{3,1},{5,3},{7,5},{10,8},{12,10},{14,12},{11,9},... | collective-permute-start | bytes 3145736 | tf_op jit(solution)/shard_map/ppermute | solution.py:320
  28.8 48.3 %collective-permute-start.14 = (bf16[128,4096]{1,0:T(8,128)(2,1)S(1)}, bf16[128,4096]{1,0:T(8,128)(2,1)}, u32[]{:S(2)}, u32[]{:S(2)}) collective-permute-start(bf16[128,4096]{1,0:T(8,128)(2,1)S(1)} %collective-permute-done.13.refs_2_.refs_6_), channel_id=1, source_target_pairs={{2,4},{4,6},{3,5},{5,7},{10,12},{12,14},{11,13},{13,15},{18,20},{2... | collective-permute-start | bytes 3145736 | tf_op jit(solution)/shard_map/ppermute | solution.py:320
  33.2 43.9 %collective-permute-start.12 = (bf16[128,4096]{1,0:T(8,128)(2,1)}, bf16[128,4096]{1,0:T(8,128)(2,1)}, u32[]{:S(2)}, u32[]{:S(2)}) collective-permute-start(bf16[128,4096]{1,0:T(8,128)(2,1)} %collective-permute-done.11.refs_1_), channel_id=1, source_target_pairs={{2,0},{4,2},{3,1},{5,3},{10,8},{12,10},{11,9},{13,11},{18,16},{20,... | collective-permute-start | bytes 3145736 | tf_op jit(solution)/shard_map/ppermute | solution.py:320
  52.2 42.9 %collective-permute-start.2 = (bf16[512,1024]{1,0:T(8,128)(2,1)}, bf16[512,1024]{1,0:T(8,128)(2,1)}, u32[]{:S(2)}, u32[]{:S(2)}) collective-permute-start(bf16[512,1024]{1,0:T(8,128)(2,1)} %after.2.left), channel_id=1, source_target_pairs={{0,2},{6,4},{1,3},{7,5},{8,10},{14,12},{9,11},{15,13},{16,18},{22,... | collective-permute-start | bytes 3145736 | tf_op jit(solution)/shard_map/ppermute | solution.py:359
  73.8 22.6 %collective-permute-start.7 = (bf16[128,4096]{1,0:T(8,128)(2,1)}, bf16[128,4096]{1,0:T(8,128)(2,1)S(1)}, u32[]{:S(2)}, u32[]{:S(2)}) collective-permute-start(bf16[128,4096]{1,0:T(8,128)(2,1)} %collective-permute-done.6.refs_9_.refs_13_), channel_id=1, source_target_pairs={{2,4},{4,6},{3,5},{5,7},{10,12},{12,14},{11,13},{13,15},{18,20},{2... | collective-permute-start | bytes 3145736 | tf_op jit(solution)/shard_map/ppermute | solution.py:320
  75.2 25.8 %collective-permute-start.5 = (bf16[128,4096]{1,0:T(8,128)(2,1)}, bf16[128,4096]{1,0:T(8,128)(2,1)S(1)}, u32[]{:S(2)}, u32[]{:S(2)}) collective-permute-start(bf16[128,4096]{1,0:T(8,128)(2,1)} %collective-permute-done.4.refs_8_), channel_id=1, source_target_pairs={{2,0},{4,2},{3,1},{5,3},{10,8},{12,10},{11,9},{13,11},{18,16},{20,... | collective-permute-start | bytes 3145736 | tf_op jit(solution)/shard_map/ppermute | solution.py:320
  79.5 44.0 %collective-permute-start.15 = (bf16[128,4096]{1,0:T(8,128)(2,1)}, bf16[128,4096]{1,0:T(8,128)(2,1)S(1)}, u32[]{:S(2)}, u32[]{:S(2)}) collective-permute-start(bf16[128,4096]{1,0:T(8,128)(2,1)} %broadcast_select_fusion.1), channel_id=1, source_target_pairs={{2,0},{4,6},{3,1},{5,7},{10,8},{12,14},{11,9},{13,15},{18,16},{20,... | collective-permute-start | bytes 3145736 | tf_op jit(solution)/shard_map/ppermute | solution.py:353
  95.2 33.9 %collective-permute-start.3 = (bf16[512,1024]{1,0:T(8,128)(2,1)}, bf16[512,1024]{1,0:T(8,128)(2,1)}, u32[]{:S(2)}, u32[]{:S(2)}) collective-permute-start(bf16[512,1024]{1,0:T(8,128)(2,1)} %after.3.left), channel_id=1, source_target_pairs={{0,2},{6,4},{1,3},{7,5},{8,10},{14,12},{9,11},{15,13},{16,18},{22,... | collective-permute-start | bytes 3145736 | tf_op jit(solution)/shard_map/ppermute | solution.py:359
  104.6 28.2 %collective-permute-start.8 = (bf16[512,1024]{1,0:T(8,128)(2,1)}, bf16[512,1024]{1,0:T(8,128)(2,1)S(1)}, u32[]{:S(2)}, u32[]{:S(2)}) collective-permute-start(bf16[512,1024]{1,0:T(8,128)(2,1)} %add_wide.11.left), channel_id=1, source_target_pairs={{2,4},{4,2},{3,5},{5,3},{10,12},{12,10},{11,13},{13,11},{18,20},{2... | collective-permute-start | bytes 3145736 | tf_op jit(solution)/shard_map/ppermute | solution.py:365
  110.1 38.1 %collective-permute-start.17 = (bf16[128,4096]{1,0:T(8,128)(2,1)}, bf16[128,4096]{1,0:T(8,128)(2,1)S(1)}, u32[]{:S(2)}, u32[]{:S(2)}) collective-permute-start(bf16[128,4096]{1,0:T(8,128)(2,1)} %broadcast_select_fusion), channel_id=1, source_target_pairs={{2,0},{4,6},{3,1},{5,7},{10,8},{12,14},{11,9},{13,15},{18,16},{20,... | collective-permute-start | bytes 3145736 | tf_op jit(solution)/shard_map/ppermute | solution.py:354
  127.1 28.2 %collective-permute-start.16 = (bf16[512,1024]{1,0:T(8,128)(2,1)}, bf16[512,1024]{1,0:T(8,128)(2,1)S(1)}, u32[]{:S(2)}, u32[]{:S(2)}) collective-permute-start(bf16[512,1024]{1,0:T(8,128)(2,1)} %add_wide.14.left), channel_id=1, source_target_pairs={{2,4},{4,2},{3,5},{5,3},{10,12},{12,10},{11,13},{13,11},{18,20},{2... | collective-permute-start | bytes 3145736 | tf_op jit(solution)/shard_map/ppermute | solution.py:365
  136.4 51.4 %collective-permute-start.9 = (bf16[512,1024]{1,0:T(8,128)(2,1)}, bf16[512,1024]{1,0:T(8,128)(2,1)S(1)}, u32[]{:S(2)}, u32[]{:S(2)}) collective-permute-start(bf16[512,1024]{1,0:T(8,128)(2,1)} %add_wide.12.left), channel_id=1, source_target_pairs={{2,4},{4,2},{3,5},{5,3},{10,12},{12,10},{11,13},{13,11},{18,20},{2... | collective-permute-start | bytes 3145736 | tf_op jit(solution)/shard_map/ppermute | solution.py:365
  142.2 67.3 %collective-permute-start.19 = (bf16[512,1024]{1,0:T(8,128)(2,1)}, bf16[512,1024]{1,0:T(8,128)(2,1)}, u32[]{:S(2)}, u32[]{:S(2)}) collective-permute-start(bf16[512,1024]{1,0:T(8,128)(2,1)} %add_wide.16.held), channel_id=1, source_target_pairs={{2,0},{4,6},{3,1},{5,7},{10,8},{12,14},{11,9},{13,15},{18,16},{20,... | collective-permute-start | bytes 3145736 | tf_op jit(solution)/shard_map/ppermute | solution.py:414
  146.9 50.0 %collective-permute-start.21 = (bf16[512,512]{1,0:T(8,128)(2,1)}, bf16[512,512]{1,0:T(8,128)(2,1)}, u32[]{:S(2)}, u32[]{:S(2)}) collective-permute-start(bf16[512,512]{1,0:T(8,128)(2,1)} %convolution_convert_fusion.3.left), channel_id=1, source_target_pairs={{0,2},{6,4},{1,3},{7,5},{8,10},{14,12},{9,11},{15,13},{16,18},{22,... | collective-permute-start | bytes 1572872 | tf_op jit(solution)/shard_map/ppermute | solution.py:359
  158.9 63.5 %collective-permute-start.18 = (bf16[512,1024]{1,0:T(8,128)(2,1)}, bf16[512,1024]{1,0:T(8,128)(2,1)S(1)}, u32[]{:S(2)}, u32[]{:S(2)}) collective-permute-start(bf16[512,1024]{1,0:T(8,128)(2,1)} %add_wide.15.held), channel_id=1, source_target_pairs={{2,0},{4,6},{3,1},{5,7},{10,8},{12,14},{11,9},{13,15},{18,16},{20,... | collective-permute-start | bytes 3145736 | tf_op jit(solution)/shard_map/ppermute | solution.py:414
  162.7 39.6 %collective-permute-start = (bf16[512,512]{1,0:T(8,128)(2,1)}, bf16[512,512]{1,0:T(8,128)(2,1)}, u32[]{:S(2)}, u32[]{:S(2)}) collective-permute-start(bf16[512,512]{1,0:T(8,128)(2,1)} %convolution_convert_fusion.4.left), channel_id=1, source_target_pairs={{0,2},{6,4},{1,3},{7,5},{8,10},{14,12},{9,11},{15,13},{16,18},{22,... | collective-permute-start | bytes 1572872 | tf_op jit(solution)/shard_map/ppermute | solution.py:359
  191.5 45.3 %collective-permute-start.24 = (bf16[512,1024]{1,0:T(8,128)(2,1)}, bf16[512,1024]{1,0:T(8,128)(2,1)S(1)}, u32[]{:S(2)}, u32[]{:S(2)}) collective-permute-start(bf16[512,1024]{1,0:T(8,128)(2,1)} %add_wide.20.held), channel_id=1, source_target_pairs={{2,0},{4,6},{3,1},{5,7},{10,8},{12,14},{11,9},{13,15},{18,16},{20,... | collective-permute-start | bytes 3145736 | tf_op jit(solution)/shard_map/ppermute | solution.py:414
  199.0 19.2 %collective-permute-start.22 = (bf16[512,512]{1,0:T(8,128)(2,1)}, bf16[512,512]{1,0:T(8,128)(2,1)}, u32[]{:S(2)}, u32[]{:S(2)}) collective-permute-start(bf16[512,512]{1,0:T(8,128)(2,1)} %add_wide.18.left), channel_id=1, source_target_pairs={{2,4},{4,2},{3,5},{5,3},{10,12},{12,10},{11,13},{13,11},{18,20},{2... | collective-permute-start | bytes 1572872 | tf_op jit(solution)/shard_map/ppermute | solution.py:365
  204.4 28.1 %collective-permute-start.10 = (bf16[512,512]{1,0:T(8,128)(2,1)}, bf16[512,512]{1,0:T(8,128)(2,1)S(1)}, u32[]{:S(2)}, u32[]{:S(2)}) collective-permute-start(bf16[512,512]{1,0:T(8,128)(2,1)} %add_wide.13.left), channel_id=1, source_target_pairs={{2,4},{4,2},{3,5},{5,3},{10,12},{12,10},{11,13},{13,11},{18,20},{2... | collective-permute-start | bytes 1572872 | tf_op jit(solution)/shard_map/ppermute | solution.py:365
  220.3 26.5 %collective-permute-start.23 = (bf16[512,512]{1,0:T(8,128)(2,1)}, bf16[512,512]{1,0:T(8,128)(2,1)}, u32[]{:S(2)}, u32[]{:S(2)}) collective-permute-start(bf16[512,512]{1,0:T(8,128)(2,1)} %add_wide.19.held), channel_id=1, source_target_pairs={{2,0},{4,6},{3,1},{5,7},{10,8},{12,14},{11,9},{13,15},{18,16},{20,... | collective-permute-start | bytes 1572872 | tf_op jit(solution)/shard_map/ppermute | solution.py:414
  (19 other events, 158.1 us)

commit v2 on v1

--- a/solution.py
+++ b/solution.py
@@ -35,45 +35,13 @@
     return moved, fresh
 
 
-def add_kernel(left, right, *rest):
-    total = rest[-1]
-    rows = min(128, left.shape[0])
-
-    @pl.loop(0, left.shape[0] // rows)
-    def _(step):
-        at = pl.ds(pl.multiple_of(step * rows, rows), rows)
-        total[at, :] = left[at, :] + right[at, :]
+def after(value, *ties):
+    return lax.optimization_barrier((value, *ties))[0]
 
 
 def add_wide(left, right, ties=()):
-    return pl.pallas_call(
-        add_kernel,
-        in_specs=[pl.BlockSpec(memory_space=pltpu.VMEM)] * 2
-        + [pl.BlockSpec(memory_space=pl.ANY)] * len(ties),
-        out_specs=pl.BlockSpec(memory_space=pltpu.VMEM),
-        out_shape=jax.ShapeDtypeStruct(left.shape, jnp.bfloat16),
-        cost_estimate=pl.CostEstimate(
-            flops=left.size, bytes_accessed=6 * left.size, transcendentals=0
-        ),
-        name="add_wide",
-    )(left, right, *ties)
-
-
-def same_kernel(*refs):
-    del refs
-
-
-def after(value, *ties):
-    anywhere = pl.BlockSpec(memory_space=pl.ANY)
-    return pl.pallas_call(
-        same_kernel,
-        in_specs=[anywhere] * (1 + len(ties)),
-        out_specs=anywhere,
-        out_shape=jax.ShapeDtypeStruct(value.shape, value.dtype),
-        input_output_aliases={0: 0},
-        cost_estimate=pl.CostEstimate(flops=0, bytes_accessed=0, transcendentals=0),
-        name="after",
-    )(value, *ties)
+    right = after(right, *ties) if ties else right
+    return (left.astype(jnp.float32) + right.astype(jnp.float32)).astype(jnp.bfloat16)
 
 
 def tile_of(width, largest=512):
@@ -136,11 +104,12 @@
     new_up[...] = fresh
 
 
-def chunk_specs(start, tokens, rows, width, tile):
+def chunk_specs(start, base, tokens, rows, width, tile):
     steps = width // tile
     at = start // tile
+    there_at = (start - base) // tile
     here = pl.BlockSpec((tokens, tile), lambda j: (0, j))
-    there = pl.BlockSpec((tokens, tile), lambda j: (0, at + j))
+    there = pl.BlockSpec((tokens, tile), lambda j: (0, there_at + j))
     block = pl.BlockSpec((rows, tile), lambda j: (0, at + j))
     flag = pl.BlockSpec(memory_space=pltpu.SMEM)
     return steps, block, [flag, here, here, there, there]
@@ -171,13 +140,14 @@
             out[...] = part[at, :].astype(jnp.bfloat16)
 
 
-def part_step(start, hidden, factors, weights, part, axis):
+def part_step(start, hidden, factored, weights, part, axis):
     received, held, flag = hidden
+    base, factors = factored
     tokens, width = held.shape
     rows = weights[0].shape[0]
     halves = lax.axis_size(axis) == 2
     tile = tile_of(width)
-    steps, block, in_specs = chunk_specs(start, tokens, rows, width, tile)
+    steps, block, in_specs = chunk_specs(start, base, tokens, rows, width, tile)
     whole = pl.BlockSpec((tokens, rows), lambda j: (0, 0))
     half = pl.BlockSpec((tokens // 2, rows), lambda j: (0, 0))
     index = lax.axis_index(axis).astype(jnp.int32).reshape((1,))
@@ -200,13 +170,14 @@
     )(index, flag, received, held, *factors, *weights, part)
 
 
-def update_step(kick_scale, start, hidden, factors, inputs_t, arrays, part, made, with_part):
+def update_step(kick_scale, start, hidden, factored, inputs_t, arrays, part, made, with_part):
     received, held, flag = hidden
+    base, factors = factored
     tokens, width = held.shape
     rows, columns = arrays[0].shape
     tile = tile_of(width, 512 if with_part else 256)
     first = part is None
-    steps, block, in_specs = chunk_specs(start, tokens, rows, width, tile)
+    steps, block, in_specs = chunk_specs(start, base, tokens, rows, width, tile)
     whole_inputs = pl.BlockSpec((rows, tokens), lambda j: (0, 0))
     whole_part = pl.BlockSpec((tokens, rows), lambda j: (0, 0))
     in_specs += [whole_inputs] + [block] * 6
@@ -252,7 +223,7 @@
     gate_pieces = refs[: 2 * size - 1]
     up_pieces = refs[2 * size - 1 : 4 * size - 2]
     grads, weight, momentum, noise = refs[4 * size - 2 : 4 * size + 2]
-    new_down, next_down, gate_factor, up_factor, hidden = refs[4 * size + 2 :]
+    new_down, next_down, gate_factor, up_factor, hidden = refs[-5:]
     rows = gate_pieces[0].shape[0]
 
     def piece(pieces, at):
@@ -279,22 +250,31 @@
     new_down[...] = fresh
 
 
-def saved_step(kick_scale, size, table, gate_pieces, up_pieces, grads, weight, momentum, noise):
-    rows, width = gate_pieces[0][0].shape
+def saved_step(
+    kick_scale, start, stop, table, gate_pieces, up_pieces, grads, weight, momentum, noise, made
+):
+    size = table.shape[0] // 2
+    rows = gate_pieces[0][0].shape[0]
     tokens, columns = grads.shape
+    width = stop - start
     tile = tile_of(width)
+    first = start // tile
     pieces = [*gate_pieces, *up_pieces]
-    piece_specs = [pl.BlockSpec((rows, tile), lambda j, at=at: (at, j)) for _, at in pieces]
-    block = pl.BlockSpec((tile, columns), lambda j: (j, 0))
+    piece_specs = [pl.BlockSpec((rows, tile), lambda j, at=at: (at, first + j)) for _, at in pieces]
+    block = pl.BlockSpec((tile, columns), lambda j: (first + j, 0))
     whole = pl.BlockSpec((tokens, columns), lambda j: (0, 0))
     factor = pl.BlockSpec((tokens, tile), lambda j: (0, j))
-    return pl.pallas_call(
+    operands = [table, *[array for array, _ in pieces], grads, weight, momentum, noise]
+    in_specs = [pl.BlockSpec(memory_space=pltpu.SMEM), *piece_specs, whole] + [block] * 3
+    aliases = {}
+    if made is not None:
+        aliases = {len(operands) + i: i for i in range(2)}
+        in_specs += [pl.BlockSpec(memory_space=pl.ANY)] * 2
+        operands += made
+    outs = pl.pallas_call(
         functools.partial(saved_kernel, kick_scale, size),
         grid=(width // tile,),
-        in_specs=[pl.BlockSpec(memory_space=pltpu.SMEM)]
-        + piece_specs
-        + [whole]
-        + [block] * 3,
+        in_specs=in_specs,
         out_specs=[block, block, factor, factor],
         out_shape=[
             jax.ShapeDtypeStruct(weight.shape, jnp.bfloat16),
@@ -303,6 +283,7 @@
             jax.ShapeDtypeStruct((tokens, width), jnp.bfloat16),
         ],
         scratch_shapes=[pltpu.VMEM((tokens, tile), jnp.bfloat16)],
+        input_output_aliases=aliases,
         compiler_params=pltpu.CompilerParams(vmem_limit_bytes=VMEM_LIMIT),
         cost_estimate=pl.CostEstimate(
             flops=2 * tokens * width * columns,
@@ -310,7 +291,8 @@
             transcendentals=tokens * width,
         ),
         name="saved_step",
-    )(table, *[array for array, _ in pieces], grads, weight, momentum, noise)
+    )(*operands)
+    return tuple(outs[:2]), tuple(outs[2:])
 
 
 def relay_step(behind, ahead, axis, step):
@@ -343,7 +325,7 @@
 MIDDLE = ((1, 2), (2, 1))
 
 
-def relayed_by_four(arrays, terms, axis):
+def relayed_by_four(arrays, terms, axis, early):
     me = lax.axis_index(axis).astype(jnp.int32)
     gate, up = arrays
     gate_b1, gate_a1 = relay_step(gate, gate, axis, 1)
@@ -352,10 +334,9 @@
     up_b2, up_a2 = relay_step(up_b1, up_a1, axis, 2)
     gate_out3 = lax.ppermute(jnp.where(me == 1, gate_a2, gate_b2), axis, OUTWARD)
     up_out3 = lax.ppermute(jnp.where(me == 1, up_a2, up_b2), axis, OUTWARD)
-    terms, ins = list(terms), []
+    terms, ins = list(lax.optimization_barrier((*terms, early))[:-1]), []
     for at in range(len(terms)):
-        if at in (1, 2):
-            terms[at] = after(terms[at], ins[-1])
+        terms[at] = after(terms[at], ins[min(at, 3) - 1] if at else gate_b1)
         ins.append(lax.ppermute(terms[at], axis, INWARD))
     inner, mids = [], []
     sums = []
@@ -370,9 +351,9 @@
     send_inner(0, up_a2, up_b2)
     send_inner(1, gate_out3)
     send_total(0, gate_out3)
-    send_inner(2, mids[0])
+    send_inner(2, sums[0][1])
     send_total(1, up_out3)
-    send_inner(3, mids[1])
+    send_inner(3, sums[1][1])
     send_inner(4, mids[2])
     pieces = [
         [(gate, 0), (gate_a1, 0), (gate_b1, 0), (gate_a2, 0), (gate_b2, 0)],
@@ -467,35 +448,45 @@
     ]
     send_total = None
     if size == 4:
-        pieces, table, sums, send_total = relayed_by_four(saved, terms, "row")
+        pieces, table, sums, send_total = relayed_by_four(saved, terms, "row", inputs_t)
     else:
         pieces, table = relayed(saved, "row")
         sums = row_sums(terms, "row")
 
-    new_down, next_down, *factors = saved_step(
-        kick_scale,
-        size,
-        table,
-        *pieces,
-        grads_full,
-        down_local,
-        momentum_down[0],
-        noise_down[0],
-    )
+    middle = starts[2]
+    factored, downs = [], None
+    for start, stop in ((0, middle), (middle, stops[-1])):
+        if start and sums:
+            table = after(table, sums[1][1])
+        downs, factors = saved_step(
+            kick_scale,
+            start,
+            stop,
+            table,
+            *pieces,
+            grads_full,
+            down_local,
+            momentum_down[0],
+            noise_down[0],
+            downs,
+        )
+        factored.append((start, factors))
+    new_down, next_down = downs
     weights = (gate_weight[0], up_weight[0])
     arrays = weights + (momentum_gate[0], momentum_up[0], noise_gate[0], noise_up[0])
     if send_total is not None:
-        send_total(2, factors[0])
+        send_total(2, factored[1][1][0])
     part, made = None, None
     for at, start in enumerate(starts[:-1]):
         part, made = update_step(
-            kick_scale, start, sums[at], factors, inputs_t, arrays, part, made, True
+            kick_scale, start, sums[at], factored[at > 1], inputs_t, arrays, part, made, True
         )
-        if at < 2 and send_total is not None:
-            send_total(3 + at, part)
-    parts = part_step(starts[-1], sums[-1], factors, weights, part, "col")
+        if at == 0 and send_total is not None:
+            send_total(3, part)
+            send_total(4, sums[3][1])
+    parts = part_step(starts[-1], sums[-1], factored[1], weights, part, "col")
     _, made = update_step(
-        kick_scale, starts[-1], sums[-1], factors, inputs_t, arrays, None, made, False
+        kick_scale, starts[-1], sums[-1], factored[1], inputs_t, arrays, None, made, False
     )
     new_gate, new_up, next_gate, next_up = made
     input_grad = parts_sum(parts, "col")

time: 276 us -> 253 us (0.917); the launches traced: 274 us -> 248 us
  waiting for transfers between devices: 85.6 us -> 51.9 us
  starting transfers between devices: 61.2 us -> 93.9 us
  Pallas kernels: 91.5 us -> 67.4 us
  local copies, waits for them, and re-layouts: 11.5 us -> 2.54 us
  other arithmetic: 4.66 us -> 12.5 us
    pallas_call x13 -> x0, Pallas kernels: 25.9 us -> none  [the longest x11 25.9 us: add_wide(): pl.pallas_call(add_kernel, in_specs=[pl.BlockSpec(memory_space=pltpu.VMEM...]
    ppermute x5, starting transfers between devices: 13.9 us -> 29.2 us  [send_inner(): mids.append(lax.ppermute(inner[at], axis, MIDDLE))]
    convert_element_type x0 -> x11, other arithmetic: none -> 10.1 us  [add_wide(): (left.astype(jnp.float32) + right.astype(jnp.float32)).astype(jnp.bfloat16)]
    ppermute x5, waiting for transfers between devices: 10.9 us -> 1.13 us  [send_inner(): mids.append(lax.ppermute(inner[at], axis, MIDDLE))]
    ppermute x5, waiting for transfers between devices: 24.4 us -> 15.1 us  [relayed_by_four(): ins.append(lax.ppermute(terms[at], axis, INWARD))]
    unnamed x34, local copies, waits for them, and re-layouts: 10.9 us -> 1.88 us
    ppermute x1, waiting for transfers between devices: 11.5 us -> 3.32 us  [relayed_by_four(): lax.ppermute(jnp.where(me == 1, gate_a2, gate_b2), axis, OUTWARD)]
    ppermute x8, waiting for transfers between devices: 33.4 us -> 26.9 us  [relay_step(): return (lax.ppermute(behind, axis, up), lax.ppermute(ahead, axis, down))]
  transfers between devices with their start and end apart: 27 -> 27, of which waited for: 10 -> 9; matrix products, arithmetic and copies ran while one was open for 7% -> 10% of each run, Pallas kernels for 31% -> 26%
where the time goes in v2:
time: 253 us; the launch traced here: 248 us
  starting transfers between devices  93.9 us (37%)
  Pallas kernels  67.4 us (27%)
  waiting for transfers between devices  51.9 us (21%)
  matrix products  13.6 us (5%)
  other arithmetic  12.5 us (5%)
  blocking collectives  4.69 us (2%)
  local copies, waits for them, and re-layouts  2.54 us (1%)
    pallas_call x5, Pallas kernels, update_step(): pl.pallas_call(functools.partial(update_kernel, kick_scale, with_part, fi...  38.9 us
    ppermute x5, starting transfers between devices, send_inner(): mids.append(lax.ppermute(inner[at], axis, MIDDLE))  29.2 us
    ppermute x8, waiting for transfers between devices, relay_step(): return (lax.ppermute(behind, axis, up), lax.ppermute(ahead, axis, down))  26.9 us
    ppermute x8, starting transfers between devices, relay_step(): return (lax.ppermute(behind, axis, up), lax.ppermute(ahead, axis, down))  26.7 us
    pallas_call x2, Pallas kernels, saved_step(): pl.pallas_call(functools.partial(saved_kernel, kick_scale, size), grid=(w...  24.8 us
    ppermute x5, starting transfers between devices, outward_sum(): received = lax.ppermute(held, axis, pairs)  17.3 us
    ppermute x5, waiting for transfers between devices, relayed_by_four(): ins.append(lax.ppermute(terms[at], axis, INWARD))  15.1 us
    dot_general x5, matrix products, contract(): lax.dot_general(left, right, (((left_dim,), (right_dim,)), ((), ())), pre...  13.6 us
  transfers between devices with their start and end apart: 27, of which 9 were waited for; matrix products, arithmetic and copies ran while one was open for 10% of the time, Pallas kernels for 26%

profile of v2, /device:TPU:10, one launch (start us, length us, event | category | flops | bytes accessed | tf_op | source)
XLA Modules:
  0.0 247.8 jit_solution(12465598667438762482)
XLA Ops:
  3.1 3.5 %collective-permute-start = (bf16[128,4096]{1,0:T(8,128)(2,1)}, bf16[128,4096]{1,0:T(8,128)(2,1)S(1)}, u32[]{:S(2)}, u32[]{:S(2)}) collective-permute-start(bf16[128,4096]{1,0:T(8,128)(2,1)} %bitcast.107), channel_id=1, source_target_pairs={{0,2},{2,4},{4,6},{1,3},{3,5},{5,7},{8,10},{10,12},{12,14},{9,11},... | collective-permute-start | bytes 3145736 | tf_op jit(solution)/shard_map/ppermute | solution.py:302
  6.6 4.4 %collective-permute-start.7 = (bf16[128,4096]{1,0:T(8,128)(2,1)}, bf16[128,4096]{1,0:T(8,128)(2,1)S(1)}, u32[]{:S(2)}, u32[]{:S(2)}) collective-permute-start(bf16[128,4096]{1,0:T(8,128)(2,1)} %bitcast.110), channel_id=1, source_target_pairs={{0,2},{2,4},{4,6},{1,3},{3,5},{5,7},{8,10},{10,12},{12,14},{9,11},... | collective-permute-start | bytes 3145736 | tf_op jit(solution)/shard_map/ppermute | solution.py:302
  32.8 5.5 %collective-permute-start.11 = (bf16[128,4096]{1,0:T(8,128)(2,1)}, bf16[128,4096]{1,0:T(8,128)(2,1)S(1)}, u32[]{:S(2)}, u32[]{:S(2)}) collective-permute-start(bf16[128,4096]{1,0:T(8,128)(2,1)} %collective-permute-done.10.refs_1_), channel_id=1, source_target_pairs={{2,0},{4,2},{3,1},{5,3},{10,8},{12,10},{11,9},{13,11},{18,16},{20,... | collective-permute-start | bytes 3145736 | tf_op jit(solution)/shard_map/ppermute | solution.py:302
  40.7 13.1 %collective-permute-done.7.refs_9_.refs_13_ = bf16[128,4096]{1,0:T(8,128)(2,1)S(1)} collective-permute-done((bf16[128,4096]{1,0:T(8,128)(2,1)}, bf16[128,4096]{1,0:T(8,128)(2,1)S(1)}, u32[]{:S(2)}, u32[]{:S(2)}) %collective-permute-start.7) | collective-permute-done | bytes 1048608 | tf_op jit(solution)/shard_map/ppermute | solution.py:302
  53.8 4.6 %collective-permute-start.8 = (bf16[128,4096]{1,0:T(8,128)(2,1)S(1)}, bf16[128,4096]{1,0:T(8,128)(2,1)}, u32[]{:S(2)}, u32[]{:S(2)}) collective-permute-start(bf16[128,4096]{1,0:T(8,128)(2,1)S(1)} %collective-permute-done.7.refs_9_.refs_13_), channel_id=1, source_target_pairs={{2,4},{4,6},{3,5},{5,7},{10,12},{12,14},{11,13},{13,15},{18,20},{2... | collective-permute-start | bytes 3145736 | tf_op jit(solution)/shard_map/ppermute | solution.py:302
  60.4 14.6 %collective-permute-done.1 = bf16[512,1024]{1,0:T(8,128)(2,1)} collective-permute-done((bf16[512,1024]{1,0:T(8,128)(2,1)}, bf16[512,1024]{1,0:T(8,128)(2,1)}, u32[]{:S(2)}, u32[]{:S(2)}) %collective-permute-start.1) | collective-permute-done | bytes 1048608 | tf_op jit(solution)/shard_map/ppermute | solution.py:340
  76.4 6.3 %collective-permute-start.13 = (bf16[128,4096]{1,0:T(8,128)(2,1)S(1)}, bf16[128,4096]{1,0:T(8,128)(2,1)S(1)}, u32[]{:S(2)}, u32[]{:S(2)}) collective-permute-start(bf16[128,4096]{1,0:T(8,128)(2,1)S(1)} %broadcast_select_fusion.1), channel_id=1, source_target_pairs={{2,0},{4,6},{3,1},{5,7},{10,8},{12,14},{11,9},{13,15},{18,16},{20,... | collective-permute-start | bytes 3145736 | tf_op jit(solution)/shard_map/ppermute | solution.py:335
  82.6 13.7 %collective-permute-done.8.refs_11_ = bf16[128,4096]{1,0:T(8,128)(2,1)} collective-permute-done((bf16[128,4096]{1,0:T(8,128)(2,1)S(1)}, bf16[128,4096]{1,0:T(8,128)(2,1)}, u32[]{:S(2)}, u32[]{:S(2)}) %collective-permute-start.8) | collective-permute-done | bytes 1048608 | tf_op jit(solution)/shard_map/ppermute | solution.py:302
  98.3 5.9 %collective-permute-start.9 = (bf16[512,1024]{1,0:T(8,128)(2,1)S(1)}, bf16[512,1024]{1,0:T(8,128)(2,1)S(1)}, u32[]{:S(2)}, u32[]{:S(2)}) collective-permute-start(bf16[512,1024]{1,0:T(8,128)(2,1)S(1)} %add_convert_fusion.5), channel_id=1, source_target_pairs={{2,4},{4,2},{3,5},{5,3},{10,12},{12,10},{11,13},{13,11},{18,20},{2... | collective-permute-start | bytes 3145736 | tf_op jit(solution)/shard_map/ppermute | solution.py:346
  107.9 5.6 %collective-permute-start.18 = (bf16[128,4096]{1,0:T(8,128)(2,1)}, bf16[128,4096]{1,0:T(8,128)(2,1)}, u32[]{:S(2)}, u32[]{:S(2)}) collective-permute-start(bf16[128,4096]{1,0:T(8,128)(2,1)} %broadcast_select_fusion), channel_id=1, source_target_pairs={{2,0},{4,6},{3,1},{5,7},{10,8},{12,14},{11,9},{13,15},{18,16},{20,... | collective-permute-start | bytes 3145736 | tf_op jit(solution)/shard_map/ppermute | solution.py:336
  117.2 8.0 %collective-permute-start.17 = (bf16[512,1024]{1,0:T(8,128)(2,1)S(1)}, bf16[512,1024]{1,0:T(8,128)(2,1)}, u32[]{:S(2)}, u32[]{:S(2)}) collective-permute-start(bf16[512,1024]{1,0:T(8,128)(2,1)S(1)} %add_convert_fusion.2), channel_id=1, source_target_pairs={{2,4},{4,2},{3,5},{5,3},{10,12},{12,10},{11,13},{13,11},{18,20},{2... | collective-permute-start | bytes 3145736 | tf_op jit(solution)/shard_map/ppermute | solution.py:346
  133.7 5.4 %collective-permute-start.20 = (bf16[512,1024]{1,0:T(8,128)(2,1)}, bf16[512,1024]{1,0:T(8,128)(2,1)S(1)}, u32[]{:S(2)}, u32[]{:S(2)}) collective-permute-start(bf16[512,1024]{1,0:T(8,128)(2,1)} %add_convert_fusion.4.held), channel_id=1, source_target_pairs={{2,0},{4,6},{3,1},{5,7},{10,8},{12,14},{11,9},{13,15},{18,16},{20,... | collective-permute-start | bytes 3145736 | tf_op jit(solution)/shard_map/ppermute | solution.py:395
  139.4 12.4 %saved_step.2 = (bf16[4096,512]{1,0:T(8,128)(2,1)}, f32[4096,512]{1,0:T(8,128)}, bf16[512,2048]{1,0:T(8,128)(2,1)}, bf16[512,2048]{1,0:T(8,128)(2,1)}) custom-call(s32[8]{0:T(128)} %stack.37.table, bf16[128,4096]{1,0:T(8,128)(2,1)} %bitcast.108, bf16[128,4096]{1,0:T(8,128)(2,1)} %collective-permute-done.10.refs_1_, bf16[128,4096]{1,0:T(8,128)(2,1)} %copy-done, ...), custom_call_target="tpu_custom_call" | custom-call | flops 1073741824 | bytes 27262976 | tf_op jit(solution)/shard_map/saved_step/pallas_call | solution.py:274
  153.4 5.4 %collective-permute-start.24 = (bf16[512,1024]{1,0:T(8,128)(2,1)S(1)}, bf16[512,1024]{1,0:T(8,128)(2,1)}, u32[]{:S(2)}, u32[]{:S(2)}) collective-permute-start(bf16[512,1024]{1,0:T(8,128)(2,1)S(1)} %add_convert_fusion.1.held), channel_id=1, source_target_pairs={{2,0},{4,6},{3,1},{5,7},{10,8},{12,14},{11,9},{13,15},{18,16},{20,... | collective-permute-start | bytes 3145736 | tf_op jit(solution)/shard_map/ppermute | solution.py:395
  160.1 12.4 %saved_step.3 = (bf16[4096,512]{1,0:T(8,128)(2,1)}, f32[4096,512]{1,0:T(8,128)}, bf16[512,2048]{1,0:T(8,128)(2,1)}, bf16[512,2048]{1,0:T(8,128)(2,1)}) custom-call(s32[8]{0:T(128)} %stack.37.table, bf16[128,4096]{1,0:T(8,128)(2,1)} %bitcast.109, bf16[128,4096]{1,0:T(8,128)(2,1)} %collective-permute-done.10.refs_1_, ...), custom_call_target="tpu_custom_call", output_to_operand_aliasing={{0}: (19, {}), {1}: (20, {})} | custom-call | flops 1073741824 | bytes 27262976 | tf_op jit(solution)/shard_map/saved_step/pallas_call | solution.py:274
  173.9 8.0 %collective-permute-start.19 = (bf16[512,512]{1,0:T(8,128)(2,1)S(1)}, bf16[512,512]{1,0:T(8,128)(2,1)S(1)}, u32[]{:S(2)}, u32[]{:S(2)}) collective-permute-start(bf16[512,512]{1,0:T(8,128)(2,1)S(1)} %add_convert_fusion.8), channel_id=1, source_target_pairs={{2,4},{4,2},{3,5},{5,3},{10,12},{12,10},{11,13},{13,11},{18,20},{2... | collective-permute-start | bytes 1572872 | tf_op jit(solution)/shard_map/ppermute | solution.py:346
  185.9 4.2 %collective-permute-start.15 = (bf16[512,512]{1,0:T(8,128)(2,1)S(1)}, bf16[512,512]{1,0:T(8,128)(2,1)S(1)}, u32[]{:S(2)}, u32[]{:S(2)}) collective-permute-start(bf16[512,512]{1,0:T(8,128)(2,1)S(1)} %add_convert_fusion.9), channel_id=1, source_target_pairs={{2,4},{4,2},{3,5},{5,3},{10,12},{12,10},{11,13},{13,11},{18,20},{2... | collective-permute-start | bytes 1572872 | tf_op jit(solution)/shard_map/ppermute | solution.py:346
  191.1 8.8 %update_step.5 = (bf16[512,4096]{1,0:T(8,128)(2,1)}, bf16[512,4096]{1,0:T(8,128)(2,1)}, f32[512,4096]{1,0:T(8,128)}, f32[512,4096]{1,0:T(8,128)}, f32[512,512]{1,0:T(8,128)}) custom-call(s32[1]{0:T(128)} %bitcast.1.flag, bf16[512,1024]{1,0:T(8,128)(2,1)} %copy-done.13, bf16[512,1024]{1,0:T(8,128)(2,1)} %add_convert_fusion.4.held, ...), custom_call_target="tpu_custom_call" | custom-call | flops 2147483648 | bytes 18874368 | tf_op jit(solution)/shard_map/update_step/pallas_call | solution.py:204
  204.4 9.2 %update_step.6 = (bf16[512,4096]{1,0:T(8,128)(2,1)}, bf16[512,4096]{1,0:T(8,128)(2,1)}, f32[512,4096]{1,0:T(8,128)}, f32[512,4096]{1,0:T(8,128)}, f32[512,512]{1,0:T(8,128)}) custom-call(s32[1]{0:T(128)} %bitcast.1.flag, ...), custom_call_target="tpu_custom_call", output_to_operand_aliasing={{0}: (13, {}), {1}: (14, {}), {2}: (15, {}), {3}: (16, {})} | custom-call | flops 2147483648 | bytes 18874368 | tf_op jit(solution)/shard_map/update_step/pallas_call | solution.py:204
  213.6 9.0 %update_step.7 = (bf16[512,4096]{1,0:T(8,128)(2,1)}, bf16[512,4096]{1,0:T(8,128)(2,1)}, f32[512,4096]{1,0:T(8,128)}, f32[512,4096]{1,0:T(8,128)}, f32[512,512]{1,0:T(8,128)}) custom-call(s32[1]{0:T(128)} %bitcast.1.flag, ...), custom_call_target="tpu_custom_call", output_to_operand_aliasing={{0}: (13, {}), {1}: (14, {}), {2}: (15, {}), {3}: (16, {})} | custom-call | flops 2147483648 | bytes 18874368 | tf_op jit(solution)/shard_map/update_step/pallas_call | solution.py:204
  222.7 6.7 %update_step.8 = (bf16[512,4096]{1,0:T(8,128)(2,1)}, bf16[512,4096]{1,0:T(8,128)(2,1)}, f32[512,4096]{1,0:T(8,128)}, f32[512,4096]{1,0:T(8,128)}, f32[512,512]{1,0:T(8,128)}) custom-call(s32[1]{0:T(128)} %bitcast.1.flag, ...), custom_call_target="tpu_custom_call", output_to_operand_aliasing={{0}: (13, {}), {1}: (14, {}), {2}: (15, {}), {3}: (16, {})} | custom-call | flops 1073741824 | bytes 9437184 | tf_op jit(solution)/shard_map/update_step/pallas_call | solution.py:204
  229.4 3.8 %part_step.1 = (bf16[256,512]{1,0:T(8,128)(2,1)}, bf16[256,512]{1,0:T(8,128)(2,1)}) custom-call(s32[1]{0:T(128)} %bitcast.col, s32[1]{0:T(128)} %bitcast.1.flag, bf16[512,512]{1,0:T(8,128)(2,1)} %collective-permute-done.21.received, bf16[512,512]{1,0:T(8,128)(2,1)} %copy-done.4, bf16[512,2048]{1,0:T(8,128)(2,1)} %get-tuple-element.87.gate_factor, ...), custom_call_target="tpu_custom_call" | custom-call | flops 536870912 | bytes 4718592 | tf_op jit(solution)/shard_map/part_step/pallas_call | solution.py:154
  238.4 5.1 %update_step.9 = (bf16[512,4096]{1,0:T(8,128)(2,1)}, bf16[512,4096]{1,0:T(8,128)(2,1)}, f32[512,4096]{1,0:T(8,128)}, f32[512,4096]{1,0:T(8,128)}) custom-call(s32[1]{0:T(128)} %bitcast.1.flag, bf16[512,512]{1,0:T(8,128)(2,1)} %collective-permute-done.21.received, ...), custom_call_target="tpu_custom_call", output_to_operand_aliasing={{0}: (12, {}), {1}: (13, {}), {2}: (14, {}), {3}: (15, {})} | custom-call | flops 536870912 | bytes 9437184 | tf_op jit(solution)/shard_map/update_step/pallas_call | solution.py:204
  243.6 3.6 %collective-permute-done.26 = bf16[256,512]{1,0:T(8,128)(2,1)S(1)} collective-permute-done((bf16[256,512]{1,0:T(8,128)(2,1)S(1)}, bf16[256,512]{1,0:T(8,128)(2,1)S(1)}, u32[]{:S(2)}, u32[]{:S(2)}) %collective-permute-start.26) | collective-permute-done | bytes 262176 | tf_op jit(solution)/shard_map/ppermute | solution.py:19
  (93 shorter events, 67.5 us)
Async XLA Ops:
  0.6 32.1 %collective-permute-start.10 = (bf16[128,4096]{1,0:T(8,128)(2,1)}, bf16[128,4096]{1,0:T(8,128)(2,1)}, u32[]{:S(2)}, u32[]{:S(2)}) collective-permute-start(bf16[128,4096]{1,0:T(8,128)(2,1)} %bitcast.106), channel_id=1, source_target_pairs={{2,0},{4,2},{6,4},{3,1},{5,3},{7,5},{10,8},{12,10},{14,12},{11,9},... | collective-permute-start | bytes 3145736 | tf_op jit(solution)/shard_map/ppermute | solution.py:302
  3.1 28.4 %collective-permute-start = (bf16[128,4096]{1,0:T(8,128)(2,1)}, bf16[128,4096]{1,0:T(8,128)(2,1)S(1)}, u32[]{:S(2)}, u32[]{:S(2)}) collective-permute-start(bf16[128,4096]{1,0:T(8,128)(2,1)} %bitcast.107), channel_id=1, source_target_pairs={{0,2},{2,4},{4,6},{1,3},{3,5},{5,7},{8,10},{10,12},{12,14},{9,11},... | collective-permute-start | bytes 3145736 | tf_op jit(solution)/shard_map/ppermute | solution.py:302
  6.6 47.2 %collective-permute-start.7 = (bf16[128,4096]{1,0:T(8,128)(2,1)}, bf16[128,4096]{1,0:T(8,128)(2,1)S(1)}, u32[]{:S(2)}, u32[]{:S(2)}) collective-permute-start(bf16[128,4096]{1,0:T(8,128)(2,1)} %bitcast.110), channel_id=1, source_target_pairs={{0,2},{2,4},{4,6},{1,3},{3,5},{5,7},{8,10},{10,12},{12,14},{9,11},... | collective-permute-start | bytes 3145736 | tf_op jit(solution)/shard_map/ppermute | solution.py:302
  11.1 47.3 %collective-permute-start.5 = (bf16[128,4096]{1,0:T(8,128)(2,1)}, bf16[128,4096]{1,0:T(8,128)(2,1)}, u32[]{:S(2)}, u32[]{:S(2)}) collective-permute-start(bf16[128,4096]{1,0:T(8,128)(2,1)} %bitcast.111), channel_id=1, source_target_pairs={{2,0},{4,2},{6,4},{3,1},{5,3},{7,5},{10,8},{12,10},{14,12},{11,9},... | collective-permute-start | bytes 3145736 | tf_op jit(solution)/shard_map/ppermute | solution.py:302
  31.5 43.4 %collective-permute-start.1 = (bf16[512,1024]{1,0:T(8,128)(2,1)}, bf16[512,1024]{1,0:T(8,128)(2,1)}, u32[]{:S(2)}, u32[]{:S(2)}) collective-permute-start(bf16[512,1024]{1,0:T(8,128)(2,1)} %convolution_convert_fusion.2), channel_id=1, source_target_pairs={{0,2},{6,4},{1,3},{7,5},{8,10},{14,12},{9,11},{15,13},{16,18},{22,... | collective-permute-start | bytes 3145736 | tf_op jit(solution)/shard_map/ppermute | solution.py:340
  32.8 43.4 %collective-permute-start.11 = (bf16[128,4096]{1,0:T(8,128)(2,1)}, bf16[128,4096]{1,0:T(8,128)(2,1)S(1)}, u32[]{:S(2)}, u32[]{:S(2)}) collective-permute-start(bf16[128,4096]{1,0:T(8,128)(2,1)} %collective-permute-done.10.refs_1_), channel_id=1, source_target_pairs={{2,0},{4,2},{3,1},{5,3},{10,8},{12,10},{11,9},{13,11},{18,16},{20,... | collective-permute-start | bytes 3145736 | tf_op jit(solution)/shard_map/ppermute | solution.py:302
  38.3 37.9 %collective-permute-start.12 = (bf16[128,4096]{1,0:T(8,128)(2,1)S(1)}, bf16[128,4096]{1,0:T(8,128)(2,1)}, u32[]{:S(2)}, u32[]{:S(2)}) collective-permute-start(bf16[128,4096]{1,0:T(8,128)(2,1)S(1)} %collective-permute-done.refs_2_.refs_6_), channel_id=1, source_target_pairs={{2,4},{4,6},{3,5},{5,7},{10,12},{12,14},{11,13},{13,15},{18,20},{2... | collective-permute-start | bytes 3145736 | tf_op jit(solution)/shard_map/ppermute | solution.py:302
  53.8 42.6 %collective-permute-start.8 = (bf16[128,4096]{1,0:T(8,128)(2,1)S(1)}, bf16[128,4096]{1,0:T(8,128)(2,1)}, u32[]{:S(2)}, u32[]{:S(2)}) collective-permute-start(bf16[128,4096]{1,0:T(8,128)(2,1)S(1)} %collective-permute-done.7.refs_9_.refs_13_), channel_id=1, source_target_pairs={{2,4},{4,6},{3,5},{5,7},{10,12},{12,14},{11,13},{13,15},{18,20},{2... | collective-permute-start | bytes 3145736 | tf_op jit(solution)/shard_map/ppermute | solution.py:302
  58.4 38.0 %collective-permute-start.6 = (bf16[128,4096]{1,0:T(8,128)(2,1)}, bf16[128,4096]{1,0:T(8,128)(2,1)}, u32[]{:S(2)}, u32[]{:S(2)}) collective-permute-start(bf16[128,4096]{1,0:T(8,128)(2,1)} %collective-permute-done.5.refs_8_), channel_id=1, source_target_pairs={{2,0},{4,2},{3,1},{5,3},{10,8},{12,10},{11,9},{13,11},{18,16},{20,... | collective-permute-start | bytes 3145736 | tf_op jit(solution)/shard_map/ppermute | solution.py:302
  74.9 29.3 %collective-permute-start.2 = (bf16[512,1024]{1,0:T(8,128)(2,1)}, bf16[512,1024]{1,0:T(8,128)(2,1)S(1)}, u32[]{:S(2)}, u32[]{:S(2)}) collective-permute-start(bf16[512,1024]{1,0:T(8,128)(2,1)} %convolution_convert_fusion.1), channel_id=1, source_target_pairs={{0,2},{6,4},{1,3},{7,5},{8,10},{14,12},{9,11},{15,13},{16,18},{22,... | collective-permute-start | bytes 3145736 | tf_op jit(solution)/shard_map/ppermute | solution.py:340
  76.4 40.4 %collective-permute-start.13 = (bf16[128,4096]{1,0:T(8,128)(2,1)S(1)}, bf16[128,4096]{1,0:T(8,128)(2,1)S(1)}, u32[]{:S(2)}, u32[]{:S(2)}) collective-permute-start(bf16[128,4096]{1,0:T(8,128)(2,1)S(1)} %broadcast_select_fusion.1), channel_id=1, source_target_pairs={{2,0},{4,6},{3,1},{5,7},{10,8},{12,14},{11,9},{13,15},{18,16},{20,... | collective-permute-start | bytes 3145736 | tf_op jit(solution)/shard_map/ppermute | solution.py:335
  98.3 28.0 %collective-permute-start.9 = (bf16[512,1024]{1,0:T(8,128)(2,1)S(1)}, bf16[512,1024]{1,0:T(8,128)(2,1)S(1)}, u32[]{:S(2)}, u32[]{:S(2)}) collective-permute-start(bf16[512,1024]{1,0:T(8,128)(2,1)S(1)} %add_convert_fusion.5), channel_id=1, source_target_pairs={{2,4},{4,2},{3,5},{5,3},{10,12},{12,10},{11,13},{13,11},{18,20},{2... | collective-permute-start | bytes 3145736 | tf_op jit(solution)/shard_map/ppermute | solution.py:346
  104.2 23.9 %collective-permute-start.3 = (bf16[512,1024]{1,0:T(8,128)(2,1)S(1)}, bf16[512,1024]{1,0:T(8,128)(2,1)S(1)}, u32[]{:S(2)}, u32[]{:S(2)}) collective-permute-start(bf16[512,1024]{1,0:T(8,128)(2,1)S(1)} %copy-done.11), channel_id=1, source_target_pairs={{0,2},{6,4},{1,3},{7,5},{8,10},{14,12},{9,11},{15,13},{16,18},{22,... | collective-permute-start | bytes 3145736 | tf_op jit(solution)/shard_map/ppermute | solution.py:340
  107.9 31.5 %collective-permute-start.18 = (bf16[128,4096]{1,0:T(8,128)(2,1)}, bf16[128,4096]{1,0:T(8,128)(2,1)}, u32[]{:S(2)}, u32[]{:S(2)}) collective-permute-start(bf16[128,4096]{1,0:T(8,128)(2,1)} %broadcast_select_fusion), channel_id=1, source_target_pairs={{2,0},{4,6},{3,1},{5,7},{10,8},{12,14},{11,9},{13,15},{18,16},{20,... | collective-permute-start | bytes 3145736 | tf_op jit(solution)/shard_map/ppermute | solution.py:336
  117.2 34.5 %collective-permute-start.17 = (bf16[512,1024]{1,0:T(8,128)(2,1)S(1)}, bf16[512,1024]{1,0:T(8,128)(2,1)}, u32[]{:S(2)}, u32[]{:S(2)}) collective-permute-start(bf16[512,1024]{1,0:T(8,128)(2,1)S(1)} %add_convert_fusion.2), channel_id=1, source_target_pairs={{2,4},{4,2},{3,5},{5,3},{10,12},{12,10},{11,13},{13,11},{18,20},{2... | collective-permute-start | bytes 3145736 | tf_op jit(solution)/shard_map/ppermute | solution.py:346
  128.6 53.3 %collective-permute-start.14 = (bf16[512,1024]{1,0:T(8,128)(2,1)S(1)}, bf16[512,1024]{1,0:T(8,128)(2,1)}, u32[]{:S(2)}, u32[]{:S(2)}) collective-permute-start(bf16[512,1024]{1,0:T(8,128)(2,1)S(1)} %add_convert_fusion.3), channel_id=1, source_target_pairs={{2,4},{4,2},{3,5},{5,3},{10,12},{12,10},{11,13},{13,11},{18,20},{2... | collective-permute-start | bytes 3145736 | tf_op jit(solution)/shard_map/ppermute | solution.py:346
  131.8 40.8 %collective-permute-start.16 = (bf16[512,512]{1,0:T(8,128)(2,1)}, bf16[512,512]{1,0:T(8,128)(2,1)}, u32[]{:S(2)}, u32[]{:S(2)}) collective-permute-start(bf16[512,512]{1,0:T(8,128)(2,1)} %convolution_convert_fusion.4), channel_id=1, source_target_pairs={{0,2},{6,4},{1,3},{7,5},{8,10},{14,12},{9,11},{15,13},{16,18},{22,... | collective-permute-start | bytes 1572872 | tf_op jit(solution)/shard_map/ppermute | solution.py:340
  133.7 56.4 %collective-permute-start.20 = (bf16[512,1024]{1,0:T(8,128)(2,1)}, bf16[512,1024]{1,0:T(8,128)(2,1)S(1)}, u32[]{:S(2)}, u32[]{:S(2)}) collective-permute-start(bf16[512,1024]{1,0:T(8,128)(2,1)} %add_convert_fusion.4.held), channel_id=1, source_target_pairs={{2,0},{4,6},{3,1},{5,7},{10,8},{12,14},{11,9},{13,15},{18,16},{20,... | collective-permute-start | bytes 3145736 | tf_op jit(solution)/shard_map/ppermute | solution.py:395
  153.4 51.1 %collective-permute-start.24 = (bf16[512,1024]{1,0:T(8,128)(2,1)S(1)}, bf16[512,1024]{1,0:T(8,128)(2,1)}, u32[]{:S(2)}, u32[]{:S(2)}) collective-permute-start(bf16[512,1024]{1,0:T(8,128)(2,1)S(1)} %add_convert_fusion.1.held), channel_id=1, source_target_pairs={{2,0},{4,6},{3,1},{5,7},{10,8},{12,14},{11,9},{13,15},{18,16},{20,... | collective-permute-start | bytes 3145736 | tf_op jit(solution)/shard_map/ppermute | solution.py:395
  158.8 24.7 %collective-permute-start.4 = (bf16[512,512]{1,0:T(8,128)(2,1)S(1)}, bf16[512,512]{1,0:T(8,128)(2,1)S(1)}, u32[]{:S(2)}, u32[]{:S(2)}) collective-permute-start(bf16[512,512]{1,0:T(8,128)(2,1)S(1)} %copy-done.14), channel_id=1, source_target_pairs={{0,2},{6,4},{1,3},{7,5},{8,10},{14,12},{9,11},{15,13},{16,18},{22,... | collective-permute-start | bytes 1572872 | tf_op jit(solution)/shard_map/ppermute | solution.py:340
  173.9 26.1 %collective-permute-start.19 = (bf16[512,512]{1,0:T(8,128)(2,1)S(1)}, bf16[512,512]{1,0:T(8,128)(2,1)S(1)}, u32[]{:S(2)}, u32[]{:S(2)}) collective-permute-start(bf16[512,512]{1,0:T(8,128)(2,1)S(1)} %add_convert_fusion.8), channel_id=1, source_target_pairs={{2,4},{4,2},{3,5},{5,3},{10,12},{12,10},{11,13},{13,11},{18,20},{2... | collective-permute-start | bytes 1572872 | tf_op jit(solution)/shard_map/ppermute | solution.py:346
  183.5 30.1 %collective-permute-start.23 = (bf16[512,1024]{1,0:T(8,128)(2,1)S(1)}, bf16[512,1024]{1,0:T(8,128)(2,1)}, u32[]{:S(2)}, u32[]{:S(2)}) collective-permute-start(bf16[512,1024]{1,0:T(8,128)(2,1)S(1)} %add_convert_fusion.held), channel_id=1, source_target_pairs={{2,0},{4,6},{3,1},{5,7},{10,8},{12,14},{11,9},{13,15},{18,16},{20,... | collective-permute-start | bytes 3145736 | tf_op jit(solution)/shard_map/ppermute | solution.py:395
  200.1 22.6 %collective-permute-start.22 = (bf16[512,512]{1,0:T(8,128)(2,1)S(1)}, bf16[512,512]{1,0:T(8,128)(2,1)}, u32[]{:S(2)}, u32[]{:S(2)}) collective-permute-start(bf16[512,512]{1,0:T(8,128)(2,1)S(1)} %add_convert_fusion.7.held), channel_id=1, source_target_pairs={{2,0},{4,6},{3,1},{5,7},{10,8},{12,14},{11,9},{13,15},{18,16},{20,... | collective-permute-start | bytes 1572872 | tf_op jit(solution)/shard_map/ppermute | solution.py:395
  202.3 27.1 %collective-permute-start.21 = (bf16[512,512]{1,0:T(8,128)(2,1)S(1)}, bf16[512,512]{1,0:T(8,128)(2,1)}, u32[]{:S(2)}, u32[]{:S(2)}) collective-permute-start(bf16[512,512]{1,0:T(8,128)(2,1)S(1)} %add_convert_fusion.6.held), channel_id=1, source_target_pairs={{2,0},{4,6},{3,1},{5,7},{10,8},{12,14},{11,9},{13,15},{18,16},{20,... | collective-permute-start | bytes 1572872 | tf_op jit(solution)/shard_map/ppermute | solution.py:395
  (19 other events, 459.6 us)

commit v3 on v2

--- a/solution.py
+++ b/solution.py
@@ -226,21 +226,21 @@
     new_down, next_down, gate_factor, up_factor, hidden = refs[-5:]
     rows = gate_pieces[0].shape[0]
 
-    def piece(pieces, at):
+    def piece(pieces, at, flags):
         if at == 0:
             return pieces[0][...].astype(jnp.float32)
         one, other = pieces[2 * at - 1], pieces[2 * at]
         return jnp.where(
-            table[at] == 1, one[...].astype(jnp.float32), other[...].astype(jnp.float32)
+            table[flags + at] == 1, one[...].astype(jnp.float32), other[...].astype(jnp.float32)
         )
 
     for part in range(size):
-        gate_wide = piece(gate_pieces, part)
-        up_wide = piece(up_pieces, part)
+        gate_wide = piece(gate_pieces, part, 0)
+        up_wide = piece(up_pieces, part, size)
         sigmoid_gate = 0.5 + 0.5 * jnp.tanh(0.5 * gate_wide)
         silu_gate = gate_wide * sigmoid_gate
         slope = sigmoid_gate * (1.0 + gate_wide * (1.0 - sigmoid_gate))
-        at = pl.ds(pl.multiple_of(table[size + part] * rows, rows), rows)
+        at = pl.ds(pl.multiple_of(table[2 * size + part] * rows, rows), rows)
         gate_factor[at, :] = (up_wide * slope).astype(jnp.bfloat16)
         up_factor[at, :] = silu_gate.astype(jnp.bfloat16)
         hidden[at, :] = (silu_gate * up_wide).astype(jnp.bfloat16)
@@ -253,7 +253,7 @@
 def saved_step(
     kick_scale, start, stop, table, gate_pieces, up_pieces, grads, weight, momentum, noise, made
 ):
-    size = table.shape[0] // 2
+    size = table.shape[0] // 3
     rows = gate_pieces[0][0].shape[0]
     tokens, columns = grads.shape
     width = stop - start
@@ -316,7 +316,8 @@
         for back in range(1, size):
             pieces[-1] += [(behind[back], 0), (ahead[size - back], 0)]
     backs = jnp.arange(size, dtype=jnp.int32)
-    table = jnp.concatenate([(me >= backs).astype(jnp.int32), (me - backs + size) % size])
+    flags = (me >= backs).astype(jnp.int32)
+    table = jnp.concatenate([flags, flags, (me - backs + size) % size])
     return pieces, table
 
 
@@ -328,7 +329,9 @@
 def relayed_by_four(arrays, terms, axis, early):
     me = lax.axis_index(axis).astype(jnp.int32)
     gate, up = arrays
-    gate_b1, gate_a1 = relay_step(gate, gate, axis, 1)
+    gate_out1 = lax.ppermute(gate, axis, OUTWARD)
+    gate_b1 = lax.ppermute(gate, axis, [(0, 1), (1, 2)])
+    gate_a1 = after(lax.ppermute(gate, axis, [(2, 1), (3, 2)]), gate_out1)
     up_b1, up_a1 = relay_step(up, up, axis, 1)
     gate_b2, gate_a2 = relay_step(gate_b1, gate_a1, axis, 2)
     up_b2, up_a2 = relay_step(up_b1, up_a1, axis, 2)
@@ -356,13 +359,12 @@
     send_inner(3, sums[1][1])
     send_inner(4, mids[2])
     pieces = [
-        [(gate, 0), (gate_a1, 0), (gate_b1, 0), (gate_a2, 0), (gate_b2, 0)],
-        [(up, 0), (up_a1, 0), (up_b1, 0), (up_a2, 0), (up_b2, 0)],
+        [gate, gate_a1, gate_out1, gate_a2, gate_b2, gate_out3, gate_b1],
+        [up, up_a1, up_b1, up_a2, up_b2, up_out3, up_b1],
     ]
-    pieces[0] += [(gate_out3, 0), (gate_b1, 0)]
-    pieces[1] += [(up_out3, 0), (up_b1, 0)]
+    pieces = [[(array, 0) for array in group] for group in pieces]
     end = (me == 0) | (me == 3)
-    flags = [me < 3, me < 3, me < 2, end]
+    flags = [end, ~end, me < 2, end] + [end, me < 3, me < 2, end]
     places = [me, jnp.where(me < 3, me + 1, 2), (me + 2) % 4, jnp.where(end, 3 - me, me - 1)]
     table = jnp.stack([flag.astype(jnp.int32) for flag in flags] + places)
     return pieces, table, sums, send_total

time: 253 us -> 251 us (level)
  starting transfers between devices: 93.9 us -> 81.9 us
  waiting for transfers between devices: 51.9 us -> 61.9 us
    ppermute x5, starting transfers between devices: 29.2 us -> 19.9 us  [send_inner(): mids.append(lax.ppermute(inner[at], axis, MIDDLE))]
    ppermute x0 -> x3, starting transfers between devices: none -> 9.09 us  [the longest x1 5.25 us: relayed_by_four(): gate_b1 = lax.ppermute(gate, axis, [(0, 1), (1, 2)])]
    ppermute x5, waiting for transfers between devices: 1.13 us -> 9.28 us  [send_inner(): mids.append(lax.ppermute(inner[at], axis, MIDDLE))]
    ppermute x8 -> x6, starting transfers between devices: 26.7 us -> 20 us  [relay_step(): return (lax.ppermute(behind, axis, up), lax.ppermute(ahead, axis, down))]
    ppermute x8 -> x6, waiting for transfers between devices: 26.9 us -> 30.9 us  [relay_step(): return (lax.ppermute(behind, axis, up), lax.ppermute(ahead, axis, down))]
    ppermute x1, starting transfers between devices: 6.26 us -> 3.69 us  [relayed_by_four(): lax.ppermute(jnp.where(me == 1, gate_a2, gate_b2), axis, OUTWARD)]
  transfers between devices with their start and end apart: 27 -> 28, of which waited for: 9 -> 11; matrix products, arithmetic and copies ran while one was open for 10% -> 11% of each run, Pallas kernels for 26% -> 26%
where the time goes in v3:
time: 251 us; the launch traced here: 247 us
  starting transfers between devices  81.9 us (33%)
  Pallas kernels  67.6 us (27%)
  waiting for transfers between devices  61.9 us (25%)
  matrix products  13.6 us (5%)
  other arithmetic  12.5 us (5%)
  blocking collectives  4.69 us (2%)
  local copies, waits for them, and re-layouts  3.51 us (1%)
    pallas_call x5, Pallas kernels, update_step(): pl.pallas_call(functools.partial(update_kernel, kick_scale, with_part, fi...  38.9 us
    ppermute x6, waiting for transfers between devices, relay_step(): return (lax.ppermute(behind, axis, up), lax.ppermute(ahead, axis, down))  30.9 us
    pallas_call x2, Pallas kernels, saved_step(): pl.pallas_call(functools.partial(saved_kernel, kick_scale, size), grid=(w...  24.9 us
    ppermute x6, starting transfers between devices, relay_step(): return (lax.ppermute(behind, axis, up), lax.ppermute(ahead, axis, down))  20 us
    ppermute x5, starting transfers between devices, send_inner(): mids.append(lax.ppermute(inner[at], axis, MIDDLE))  19.9 us
    ppermute x5, starting transfers between devices, outward_sum(): received = lax.ppermute(held, axis, pairs)  14.8 us
    dot_general x5, matrix products, contract(): lax.dot_general(left, right, (((left_dim,), (right_dim,)), ((), ())), pre...  13.6 us
    ppermute x5, waiting for transfers between devices, relayed_by_four(): ins.append(lax.ppermute(terms[at], axis, INWARD))  12.9 us
  transfers between devices with their start and end apart: 28, of which 11 were waited for; matrix products, arithmetic and copies ran while one was open for 11% of the time, Pallas kernels for 26%

profile of v3, /device:TPU:10, one launch (start us, length us, event | category | flops | bytes accessed | tf_op | source)
XLA Modules:
  0.0 247.0 jit_solution(1416961043994681595)
XLA Ops:
  4.5 5.2 %collective-permute-start = (bf16[128,4096]{1,0:T(8,128)(2,1)}, bf16[128,4096]{1,0:T(8,128)(2,1)}, u32[]{:S(2)}, u32[]{:S(2)}) collective-permute-start(bf16[128,4096]{1,0:T(8,128)(2,1)} %bitcast.109), channel_id=1, source_target_pairs={{0,2},{2,4},{1,3},{3,5},{8,10},{10,12},{9,11},{11,13},{16,18},{18,... | collective-permute-start | bytes 3145736 | tf_op jit(solution)/shard_map/ppermute | solution.py:333
  11.7 4.0 %collective-permute-start.5 = (bf16[128,4096]{1,0:T(8,128)(2,1)}, bf16[128,4096]{1,0:T(8,128)(2,1)}, u32[]{:S(2)}, u32[]{:S(2)}) collective-permute-start(bf16[128,4096]{1,0:T(8,128)(2,1)} %bitcast.113), channel_id=1, source_target_pairs={{2,0},{4,2},{6,4},{3,1},{5,3},{7,5},{10,8},{12,10},{14,12},{11,9},... | collective-permute-start | bytes 3145736 | tf_op jit(solution)/shard_map/ppermute | solution.py:302
  36.5 5.5 %collective-permute-start.12 = (bf16[128,4096]{1,0:T(8,128)(2,1)}, bf16[128,4096]{1,0:T(8,128)(2,1)S(1)}, u32[]{:S(2)}, u32[]{:S(2)}) collective-permute-start(bf16[128,4096]{1,0:T(8,128)(2,1)} %collective-permute-done.10.refs_1_), channel_id=1, source_target_pairs={{2,0},{4,2},{3,1},{5,3},{10,8},{12,10},{11,9},{13,11},{18,16},{20,... | collective-permute-start | bytes 3145736 | tf_op jit(solution)/shard_map/ppermute | solution.py:302
  43.4 12.8 %collective-permute-done.7.refs_9_.refs_13_ = bf16[128,4096]{1,0:T(8,128)(2,1)S(1)} collective-permute-done((bf16[128,4096]{1,0:T(8,128)(2,1)}, bf16[128,4096]{1,0:T(8,128)(2,1)S(1)}, u32[]{:S(2)}, u32[]{:S(2)}) %collective-permute-start.7) | collective-permute-done | bytes 1048608 | tf_op jit(solution)/shard_map/ppermute | solution.py:302
  56.1 5.3 %collective-permute-start.8 = (bf16[128,4096]{1,0:T(8,128)(2,1)S(1)}, bf16[128,4096]{1,0:T(8,128)(2,1)}, u32[]{:S(2)}, u32[]{:S(2)}) collective-permute-start(bf16[128,4096]{1,0:T(8,128)(2,1)S(1)} %collective-permute-done.7.refs_9_.refs_13_), channel_id=1, source_target_pairs={{2,4},{4,6},{3,5},{5,7},{10,12},{12,14},{11,13},{13,15},{18,20},{2... | collective-permute-start | bytes 3145736 | tf_op jit(solution)/shard_map/ppermute | solution.py:302
  63.4 12.9 %collective-permute-done.1 = bf16[512,1024]{1,0:T(8,128)(2,1)} collective-permute-done((bf16[512,1024]{1,0:T(8,128)(2,1)}, bf16[512,1024]{1,0:T(8,128)(2,1)}, u32[]{:S(2)}, u32[]{:S(2)}) %collective-permute-start.1) | collective-permute-done | bytes 1048608 | tf_op jit(solution)/shard_map/ppermute | solution.py:343
  78.7 3.7 %collective-permute-start.14 = (bf16[128,4096]{1,0:T(8,128)(2,1)S(1)}, bf16[128,4096]{1,0:T(8,128)(2,1)S(1)}, u32[]{:S(2)}, u32[]{:S(2)}) collective-permute-start(bf16[128,4096]{1,0:T(8,128)(2,1)S(1)} %broadcast_select_fusion.1), channel_id=1, source_target_pairs={{2,0},{4,6},{3,1},{5,7},{10,8},{12,14},{11,9},{13,15},{18,16},{20,... | collective-permute-start | bytes 3145736 | tf_op jit(solution)/shard_map/ppermute | solution.py:338
  82.4 17.1 %collective-permute-done.8.refs_11_ = bf16[128,4096]{1,0:T(8,128)(2,1)} collective-permute-done((bf16[128,4096]{1,0:T(8,128)(2,1)S(1)}, bf16[128,4096]{1,0:T(8,128)(2,1)}, u32[]{:S(2)}, u32[]{:S(2)}) %collective-permute-start.8) | collective-permute-done | bytes 1048608 | tf_op jit(solution)/shard_map/ppermute | solution.py:302
  101.4 4.5 %collective-permute-start.9 = (bf16[512,1024]{1,0:T(8,128)(2,1)S(1)}, bf16[512,1024]{1,0:T(8,128)(2,1)S(1)}, u32[]{:S(2)}, u32[]{:S(2)}) collective-permute-start(bf16[512,1024]{1,0:T(8,128)(2,1)S(1)} %add_convert_fusion.5), channel_id=1, source_target_pairs={{2,4},{4,2},{3,5},{5,3},{10,12},{12,10},{11,13},{13,11},{18,20},{2... | collective-permute-start | bytes 3145736 | tf_op jit(solution)/shard_map/ppermute | solution.py:349
  109.6 5.6 %collective-permute-start.19 = (bf16[128,4096]{1,0:T(8,128)(2,1)}, bf16[128,4096]{1,0:T(8,128)(2,1)}, u32[]{:S(2)}, u32[]{:S(2)}) collective-permute-start(bf16[128,4096]{1,0:T(8,128)(2,1)} %broadcast_select_fusion), channel_id=1, source_target_pairs={{2,0},{4,6},{3,1},{5,7},{10,8},{12,14},{11,9},{13,15},{18,16},{20,... | collective-permute-start | bytes 3145736 | tf_op jit(solution)/shard_map/ppermute | solution.py:339
  117.2 4.6 %collective-permute-start.18 = (bf16[512,1024]{1,0:T(8,128)(2,1)S(1)}, bf16[512,1024]{1,0:T(8,128)(2,1)}, u32[]{:S(2)}, u32[]{:S(2)}) collective-permute-start(bf16[512,1024]{1,0:T(8,128)(2,1)S(1)} %add_convert_fusion.2), channel_id=1, source_target_pairs={{2,4},{4,2},{3,5},{5,3},{10,12},{12,10},{11,13},{13,11},{18,20},{2... | collective-permute-start | bytes 3145736 | tf_op jit(solution)/shard_map/ppermute | solution.py:349
  121.8 8.2 %collective-permute-done.9 = bf16[512,1024]{1,0:T(8,128)(2,1)S(1)} collective-permute-done((bf16[512,1024]{1,0:T(8,128)(2,1)S(1)}, bf16[512,1024]{1,0:T(8,128)(2,1)S(1)}, u32[]{:S(2)}, u32[]{:S(2)}) %collective-permute-start.9) | collective-permute-done | bytes 1048608 | tf_op jit(solution)/shard_map/ppermute | solution.py:349
  131.8 3.9 %collective-permute-start.15 = (bf16[512,1024]{1,0:T(8,128)(2,1)S(1)}, bf16[512,1024]{1,0:T(8,128)(2,1)}, u32[]{:S(2)}, u32[]{:S(2)}) collective-permute-start(bf16[512,1024]{1,0:T(8,128)(2,1)S(1)} %add_convert_fusion.3), channel_id=1, source_target_pairs={{2,4},{4,2},{3,5},{5,3},{10,12},{12,10},{11,13},{13,11},{18,20},{2... | collective-permute-start | bytes 3145736 | tf_op jit(solution)/shard_map/ppermute | solution.py:349
  137.7 5.4 %collective-permute-start.21 = (bf16[512,1024]{1,0:T(8,128)(2,1)}, bf16[512,1024]{1,0:T(8,128)(2,1)S(1)}, u32[]{:S(2)}, u32[]{:S(2)}) collective-permute-start(bf16[512,1024]{1,0:T(8,128)(2,1)} %add_convert_fusion.4.held), channel_id=1, source_target_pairs={{2,0},{4,6},{3,1},{5,7},{10,8},{12,14},{11,9},{13,15},{18,16},{20,... | collective-permute-start | bytes 3145736 | tf_op jit(solution)/shard_map/ppermute | solution.py:397
  143.1 12.4 %saved_step.2 = (bf16[4096,512]{1,0:T(8,128)(2,1)}, f32[4096,512]{1,0:T(8,128)}, bf16[512,2048]{1,0:T(8,128)(2,1)}, bf16[512,2048]{1,0:T(8,128)(2,1)}) custom-call(s32[12]{0:T(128)} %stack.48.table, bf16[128,4096]{1,0:T(8,128)(2,1)} %bitcast.110, bf16[128,4096]{1,0:T(8,128)(2,1)} %collective-permute-done.10.refs_1_, bf16[128,4096]{1,0:T(8,128)(2,1)} %copy-done.7, ...), custom_call_target="tpu_custom_call" | custom-call | flops 1073741824 | bytes 27262976 | tf_op jit(solution)/shard_map/saved_step/pallas_call | solution.py:274
  160.8 12.5 %saved_step.3 = (bf16[4096,512]{1,0:T(8,128)(2,1)}, f32[4096,512]{1,0:T(8,128)}, bf16[512,2048]{1,0:T(8,128)(2,1)}, bf16[512,2048]{1,0:T(8,128)(2,1)}) custom-call(s32[12]{0:T(128)} %stack.48.table, bf16[128,4096]{1,0:T(8,128)(2,1)} %bitcast.111, bf16[128,4096]{1,0:T(8,128)(2,1)} %collective-permute-done.10.refs_1_, ...), custom_call_target="tpu_custom_call", output_to_operand_aliasing={{0}: (19, {}), {1}: (20, {})} | custom-call | flops 1073741824 | bytes 27262976 | tf_op jit(solution)/shard_map/saved_step/pallas_call | solution.py:274
  182.7 3.5 %collective-permute-start.16 = (bf16[512,512]{1,0:T(8,128)(2,1)S(1)}, bf16[512,512]{1,0:T(8,128)(2,1)S(1)}, u32[]{:S(2)}, u32[]{:S(2)}) collective-permute-start(bf16[512,512]{1,0:T(8,128)(2,1)S(1)} %add_convert_fusion.9), channel_id=1, source_target_pairs={{2,4},{4,2},{3,5},{5,3},{10,12},{12,10},{11,13},{13,11},{18,20},{2... | collective-permute-start | bytes 1572872 | tf_op jit(solution)/shard_map/ppermute | solution.py:349
  187.2 8.8 %update_step.5 = (bf16[512,4096]{1,0:T(8,128)(2,1)}, bf16[512,4096]{1,0:T(8,128)(2,1)}, f32[512,4096]{1,0:T(8,128)}, f32[512,4096]{1,0:T(8,128)}, f32[512,512]{1,0:T(8,128)}) custom-call(s32[1]{0:T(128)} %bitcast.1.flag, bf16[512,1024]{1,0:T(8,128)(2,1)} %copy-done.14, bf16[512,1024]{1,0:T(8,128)(2,1)} %add_convert_fusion.4.held, ...), custom_call_target="tpu_custom_call" | custom-call | flops 2147483648 | bytes 18874368 | tf_op jit(solution)/shard_map/update_step/pallas_call | solution.py:204
  201.7 9.2 %update_step.6 = (bf16[512,4096]{1,0:T(8,128)(2,1)}, bf16[512,4096]{1,0:T(8,128)(2,1)}, f32[512,4096]{1,0:T(8,128)}, f32[512,4096]{1,0:T(8,128)}, f32[512,512]{1,0:T(8,128)}) custom-call(s32[1]{0:T(128)} %bitcast.1.flag, ...), custom_call_target="tpu_custom_call", output_to_operand_aliasing={{0}: (13, {}), {1}: (14, {}), {2}: (15, {}), {3}: (16, {})} | custom-call | flops 2147483648 | bytes 18874368 | tf_op jit(solution)/shard_map/update_step/pallas_call | solution.py:204
  210.9 9.0 %update_step.7 = (bf16[512,4096]{1,0:T(8,128)(2,1)}, bf16[512,4096]{1,0:T(8,128)(2,1)}, f32[512,4096]{1,0:T(8,128)}, f32[512,4096]{1,0:T(8,128)}, f32[512,512]{1,0:T(8,128)}) custom-call(s32[1]{0:T(128)} %bitcast.1.flag, ...), custom_call_target="tpu_custom_call", output_to_operand_aliasing={{0}: (13, {}), {1}: (14, {}), {2}: (15, {}), {3}: (16, {})} | custom-call | flops 2147483648 | bytes 18874368 | tf_op jit(solution)/shard_map/update_step/pallas_call | solution.py:204
  221.7 6.8 %update_step.8 = (bf16[512,4096]{1,0:T(8,128)(2,1)}, bf16[512,4096]{1,0:T(8,128)(2,1)}, f32[512,4096]{1,0:T(8,128)}, f32[512,4096]{1,0:T(8,128)}, f32[512,512]{1,0:T(8,128)}) custom-call(s32[1]{0:T(128)} %bitcast.1.flag, ...), custom_call_target="tpu_custom_call", output_to_operand_aliasing={{0}: (13, {}), {1}: (14, {}), {2}: (15, {}), {3}: (16, {})} | custom-call | flops 1073741824 | bytes 9437184 | tf_op jit(solution)/shard_map/update_step/pallas_call | solution.py:204
  228.6 3.8 %part_step.1 = (bf16[256,512]{1,0:T(8,128)(2,1)}, bf16[256,512]{1,0:T(8,128)(2,1)}) custom-call(s32[1]{0:T(128)} %bitcast.col, s32[1]{0:T(128)} %bitcast.1.flag, bf16[512,512]{1,0:T(8,128)(2,1)} %collective-permute-done.22.received, bf16[512,512]{1,0:T(8,128)(2,1)} %copy-done.4, bf16[512,2048]{1,0:T(8,128)(2,1)} %get-tuple-element.89.gate_factor, ...), custom_call_target="tpu_custom_call" | custom-call | flops 536870912 | bytes 4718592 | tf_op jit(solution)/shard_map/part_step/pallas_call | solution.py:154
  237.6 5.1 %update_step.9 = (bf16[512,4096]{1,0:T(8,128)(2,1)}, bf16[512,4096]{1,0:T(8,128)(2,1)}, f32[512,4096]{1,0:T(8,128)}, f32[512,4096]{1,0:T(8,128)}) custom-call(s32[1]{0:T(128)} %bitcast.1.flag, bf16[512,512]{1,0:T(8,128)(2,1)} %collective-permute-done.22.received, ...), custom_call_target="tpu_custom_call", output_to_operand_aliasing={{0}: (12, {}), {1}: (13, {}), {2}: (14, {}), {3}: (15, {})} | custom-call | flops 536870912 | bytes 9437184 | tf_op jit(solution)/shard_map/update_step/pallas_call | solution.py:204
  242.7 3.6 %collective-permute-done.27 = bf16[256,512]{1,0:T(8,128)(2,1)S(1)} collective-permute-done((bf16[256,512]{1,0:T(8,128)(2,1)S(1)}, bf16[256,512]{1,0:T(8,128)(2,1)S(1)}, u32[]{:S(2)}, u32[]{:S(2)}) %collective-permute-start.27) | collective-permute-done | bytes 262176 | tf_op jit(solution)/shard_map/ppermute | solution.py:19
  (97 shorter events, 72.4 us)
Async XLA Ops:
  0.6 34.8 %collective-permute-start.11 = (bf16[128,4096]{1,0:T(8,128)(2,1)}, bf16[128,4096]{1,0:T(8,128)(2,1)S(1)}, u32[]{:S(2)}, u32[]{:S(2)}) collective-permute-start(bf16[128,4096]{1,0:T(8,128)(2,1)} %bitcast.107), channel_id=1, source_target_pairs={{2,0},{4,6},{3,1},{5,7},{10,8},{12,14},{11,9},{13,15},{18,16},{20,... | collective-permute-start | bytes 3145736 | tf_op jit(solution)/shard_map/ppermute | solution.py:332
  3.2 33.3 %collective-permute-start.10 = (bf16[128,4096]{1,0:T(8,128)(2,1)}, bf16[128,4096]{1,0:T(8,128)(2,1)}, u32[]{:S(2)}, u32[]{:S(2)}) collective-permute-start(bf16[128,4096]{1,0:T(8,128)(2,1)} %bitcast.108), channel_id=1, source_target_pairs={{4,2},{6,4},{5,3},{7,5},{12,10},{14,12},{13,11},{15,13},{20,18},{2... | collective-permute-start | bytes 3145736 | tf_op jit(solution)/shard_map/ppermute | solution.py:334
  4.5 29.7 %collective-permute-start = (bf16[128,4096]{1,0:T(8,128)(2,1)}, bf16[128,4096]{1,0:T(8,128)(2,1)}, u32[]{:S(2)}, u32[]{:S(2)}) collective-permute-start(bf16[128,4096]{1,0:T(8,128)(2,1)} %bitcast.109), channel_id=1, source_target_pairs={{0,2},{2,4},{1,3},{3,5},{8,10},{10,12},{9,11},{11,13},{16,18},{18,... | collective-permute-start | bytes 3145736 | tf_op jit(solution)/shard_map/ppermute | solution.py:333
  9.8 46.4 %collective-permute-start.7 = (bf16[128,4096]{1,0:T(8,128)(2,1)}, bf16[128,4096]{1,0:T(8,128)(2,1)S(1)}, u32[]{:S(2)}, u32[]{:S(2)}) collective-permute-start(bf16[128,4096]{1,0:T(8,128)(2,1)} %bitcast.112), channel_id=1, source_target_pairs={{0,2},{2,4},{4,6},{1,3},{3,5},{5,7},{8,10},{10,12},{12,14},{9,11},... | collective-permute-start | bytes 3145736 | tf_op jit(solution)/shard_map/ppermute | solution.py:302
  11.7 49.7 %collective-permute-start.5 = (bf16[128,4096]{1,0:T(8,128)(2,1)}, bf16[128,4096]{1,0:T(8,128)(2,1)}, u32[]{:S(2)}, u32[]{:S(2)}) collective-permute-start(bf16[128,4096]{1,0:T(8,128)(2,1)} %bitcast.113), channel_id=1, source_target_pairs={{2,0},{4,2},{6,4},{3,1},{5,3},{7,5},{10,8},{12,10},{14,12},{11,9},... | collective-permute-start | bytes 3145736 | tf_op jit(solution)/shard_map/ppermute | solution.py:302
  34.2 42.1 %collective-permute-start.1 = (bf16[512,1024]{1,0:T(8,128)(2,1)}, bf16[512,1024]{1,0:T(8,128)(2,1)}, u32[]{:S(2)}, u32[]{:S(2)}) collective-permute-start(bf16[512,1024]{1,0:T(8,128)(2,1)} %convolution_convert_fusion.2), channel_id=1, source_target_pairs={{0,2},{6,4},{1,3},{7,5},{8,10},{14,12},{9,11},{15,13},{16,18},{22,... | collective-permute-start | bytes 3145736 | tf_op jit(solution)/shard_map/ppermute | solution.py:343
  36.5 41.1 %collective-permute-start.12 = (bf16[128,4096]{1,0:T(8,128)(2,1)}, bf16[128,4096]{1,0:T(8,128)(2,1)S(1)}, u32[]{:S(2)}, u32[]{:S(2)}) collective-permute-start(bf16[128,4096]{1,0:T(8,128)(2,1)} %collective-permute-done.10.refs_1_), channel_id=1, source_target_pairs={{2,0},{4,2},{3,1},{5,3},{10,8},{12,10},{11,9},{13,11},{18,16},{20,... | collective-permute-start | bytes 3145736 | tf_op jit(solution)/shard_map/ppermute | solution.py:302
  42.0 36.6 %collective-permute-start.13 = (bf16[128,4096]{1,0:T(8,128)(2,1)}, bf16[128,4096]{1,0:T(8,128)(2,1)S(1)}, u32[]{:S(2)}, u32[]{:S(2)}) collective-permute-start(bf16[128,4096]{1,0:T(8,128)(2,1)} %collective-permute-done.refs_6_), channel_id=1, source_target_pairs={{2,4},{4,6},{3,5},{5,7},{10,12},{12,14},{11,13},{13,15},{18,20},{2... | collective-permute-start | bytes 3145736 | tf_op jit(solution)/shard_map/ppermute | solution.py:302
  56.1 43.4 %collective-permute-start.8 = (bf16[128,4096]{1,0:T(8,128)(2,1)S(1)}, bf16[128,4096]{1,0:T(8,128)(2,1)}, u32[]{:S(2)}, u32[]{:S(2)}) collective-permute-start(bf16[128,4096]{1,0:T(8,128)(2,1)S(1)} %collective-permute-done.7.refs_9_.refs_13_), channel_id=1, source_target_pairs={{2,4},{4,6},{3,5},{5,7},{10,12},{12,14},{11,13},{13,15},{18,20},{2... | collective-permute-start | bytes 3145736 | tf_op jit(solution)/shard_map/ppermute | solution.py:302
  61.4 38.1 %collective-permute-start.6 = (bf16[128,4096]{1,0:T(8,128)(2,1)}, bf16[128,4096]{1,0:T(8,128)(2,1)}, u32[]{:S(2)}, u32[]{:S(2)}) collective-permute-start(bf16[128,4096]{1,0:T(8,128)(2,1)} %collective-permute-done.5.refs_8_), channel_id=1, source_target_pairs={{2,0},{4,2},{3,1},{5,3},{10,8},{12,10},{11,9},{13,11},{18,16},{20,... | collective-permute-start | bytes 3145736 | tf_op jit(solution)/shard_map/ppermute | solution.py:302
  76.3 29.7 %collective-permute-start.2 = (bf16[512,1024]{1,0:T(8,128)(2,1)}, bf16[512,1024]{1,0:T(8,128)(2,1)S(1)}, u32[]{:S(2)}, u32[]{:S(2)}) collective-permute-start(bf16[512,1024]{1,0:T(8,128)(2,1)} %convolution_convert_fusion.1), channel_id=1, source_target_pairs={{0,2},{6,4},{1,3},{7,5},{8,10},{14,12},{9,11},{15,13},{16,18},{22,... | collective-permute-start | bytes 3145736 | tf_op jit(solution)/shard_map/ppermute | solution.py:343
  78.7 38.1 %collective-permute-start.14 = (bf16[128,4096]{1,0:T(8,128)(2,1)S(1)}, bf16[128,4096]{1,0:T(8,128)(2,1)S(1)}, u32[]{:S(2)}, u32[]{:S(2)}) collective-permute-start(bf16[128,4096]{1,0:T(8,128)(2,1)S(1)} %broadcast_select_fusion.1), channel_id=1, source_target_pairs={{2,0},{4,6},{3,1},{5,7},{10,8},{12,14},{11,9},{13,15},{18,16},{20,... | collective-permute-start | bytes 3145736 | tf_op jit(solution)/shard_map/ppermute | solution.py:338
  101.4 28.6 %collective-permute-start.9 = (bf16[512,1024]{1,0:T(8,128)(2,1)S(1)}, bf16[512,1024]{1,0:T(8,128)(2,1)S(1)}, u32[]{:S(2)}, u32[]{:S(2)}) collective-permute-start(bf16[512,1024]{1,0:T(8,128)(2,1)S(1)} %add_convert_fusion.5), channel_id=1, source_target_pairs={{2,4},{4,2},{3,5},{5,3},{10,12},{12,10},{11,13},{13,11},{18,20},{2... | collective-permute-start | bytes 3145736 | tf_op jit(solution)/shard_map/ppermute | solution.py:349
  106.0 25.4 %collective-permute-start.3 = (bf16[512,1024]{1,0:T(8,128)(2,1)S(1)}, bf16[512,1024]{1,0:T(8,128)(2,1)S(1)}, u32[]{:S(2)}, u32[]{:S(2)}) collective-permute-start(bf16[512,1024]{1,0:T(8,128)(2,1)S(1)} %copy-done.12), channel_id=1, source_target_pairs={{0,2},{6,4},{1,3},{7,5},{8,10},{14,12},{9,11},{15,13},{16,18},{22,... | collective-permute-start | bytes 3145736 | tf_op jit(solution)/shard_map/ppermute | solution.py:343
  109.6 33.5 %collective-permute-start.19 = (bf16[128,4096]{1,0:T(8,128)(2,1)}, bf16[128,4096]{1,0:T(8,128)(2,1)}, u32[]{:S(2)}, u32[]{:S(2)}) collective-permute-start(bf16[128,4096]{1,0:T(8,128)(2,1)} %broadcast_select_fusion), channel_id=1, source_target_pairs={{2,0},{4,6},{3,1},{5,7},{10,8},{12,14},{11,9},{13,15},{18,16},{20,... | collective-permute-start | bytes 3145736 | tf_op jit(solution)/shard_map/ppermute | solution.py:339
  117.2 38.4 %collective-permute-start.18 = (bf16[512,1024]{1,0:T(8,128)(2,1)S(1)}, bf16[512,1024]{1,0:T(8,128)(2,1)}, u32[]{:S(2)}, u32[]{:S(2)}) collective-permute-start(bf16[512,1024]{1,0:T(8,128)(2,1)S(1)} %add_convert_fusion.2), channel_id=1, source_target_pairs={{2,4},{4,2},{3,5},{5,3},{10,12},{12,10},{11,13},{13,11},{18,20},{2... | collective-permute-start | bytes 3145736 | tf_op jit(solution)/shard_map/ppermute | solution.py:349
  131.8 46.2 %collective-permute-start.15 = (bf16[512,1024]{1,0:T(8,128)(2,1)S(1)}, bf16[512,1024]{1,0:T(8,128)(2,1)}, u32[]{:S(2)}, u32[]{:S(2)}) collective-permute-start(bf16[512,1024]{1,0:T(8,128)(2,1)S(1)} %add_convert_fusion.3), channel_id=1, source_target_pairs={{2,4},{4,2},{3,5},{5,3},{10,12},{12,10},{11,13},{13,11},{18,20},{2... | collective-permute-start | bytes 3145736 | tf_op jit(solution)/shard_map/ppermute | solution.py:349
  135.7 37.6 %collective-permute-start.17 = (bf16[512,512]{1,0:T(8,128)(2,1)}, bf16[512,512]{1,0:T(8,128)(2,1)}, u32[]{:S(2)}, u32[]{:S(2)}) collective-permute-start(bf16[512,512]{1,0:T(8,128)(2,1)} %convolution_convert_fusion.4), channel_id=1, source_target_pairs={{0,2},{6,4},{1,3},{7,5},{8,10},{14,12},{9,11},{15,13},{16,18},{22,... | collective-permute-start | bytes 1572872 | tf_op jit(solution)/shard_map/ppermute | solution.py:343
  137.7 48.5 %collective-permute-start.21 = (bf16[512,1024]{1,0:T(8,128)(2,1)}, bf16[512,1024]{1,0:T(8,128)(2,1)S(1)}, u32[]{:S(2)}, u32[]{:S(2)}) collective-permute-start(bf16[512,1024]{1,0:T(8,128)(2,1)} %add_convert_fusion.4.held), channel_id=1, source_target_pairs={{2,0},{4,6},{3,1},{5,7},{10,8},{12,14},{11,9},{13,15},{18,16},{20,... | collective-permute-start | bytes 3145736 | tf_op jit(solution)/shard_map/ppermute | solution.py:397
  157.2 44.5 %collective-permute-start.25 = (bf16[512,1024]{1,0:T(8,128)(2,1)S(1)}, bf16[512,1024]{1,0:T(8,128)(2,1)}, u32[]{:S(2)}, u32[]{:S(2)}) collective-permute-start(bf16[512,1024]{1,0:T(8,128)(2,1)S(1)} %add_convert_fusion.1.held), channel_id=1, source_target_pairs={{2,0},{4,6},{3,1},{5,7},{10,8},{12,14},{11,9},{13,15},{18,16},{20,... | collective-permute-start | bytes 3145736 | tf_op jit(solution)/shard_map/ppermute | solution.py:397
  174.7 21.4 %collective-permute-start.20 = (bf16[512,512]{1,0:T(8,128)(2,1)S(1)}, bf16[512,512]{1,0:T(8,128)(2,1)S(1)}, u32[]{:S(2)}, u32[]{:S(2)}) collective-permute-start(bf16[512,512]{1,0:T(8,128)(2,1)S(1)} %add_convert_fusion.8), channel_id=1, source_target_pairs={{2,4},{4,2},{3,5},{5,3},{10,12},{12,10},{11,13},{13,11},{18,20},{2... | collective-permute-start | bytes 1572872 | tf_op jit(solution)/shard_map/ppermute | solution.py:349
  179.7 31.2 %collective-permute-start.24 = (bf16[512,1024]{1,0:T(8,128)(2,1)S(1)}, bf16[512,1024]{1,0:T(8,128)(2,1)}, u32[]{:S(2)}, u32[]{:S(2)}) collective-permute-start(bf16[512,1024]{1,0:T(8,128)(2,1)S(1)} %add_convert_fusion.held), channel_id=1, source_target_pairs={{2,0},{4,6},{3,1},{5,7},{10,8},{12,14},{11,9},{13,15},{18,16},{20,... | collective-permute-start | bytes 3145736 | tf_op jit(solution)/shard_map/ppermute | solution.py:397
  196.2 25.5 %collective-permute-start.23 = (bf16[512,512]{1,0:T(8,128)(2,1)S(1)}, bf16[512,512]{1,0:T(8,128)(2,1)}, u32[]{:S(2)}, u32[]{:S(2)}) collective-permute-start(bf16[512,512]{1,0:T(8,128)(2,1)S(1)} %add_convert_fusion.7.held), channel_id=1, source_target_pairs={{2,0},{4,6},{3,1},{5,7},{10,8},{12,14},{11,9},{13,15},{18,16},{20,... | collective-permute-start | bytes 1572872 | tf_op jit(solution)/shard_map/ppermute | solution.py:397
  199.6 29.0 %collective-permute-start.22 = (bf16[512,512]{1,0:T(8,128)(2,1)S(1)}, bf16[512,512]{1,0:T(8,128)(2,1)}, u32[]{:S(2)}, u32[]{:S(2)}) collective-permute-start(bf16[512,512]{1,0:T(8,128)(2,1)S(1)} %add_convert_fusion.6.held), channel_id=1, source_target_pairs={{2,0},{4,6},{3,1},{5,7},{10,8},{12,14},{11,9},{13,15},{18,16},{20,... | collective-permute-start | bytes 1572872 | tf_op jit(solution)/shard_map/ppermute | solution.py:397
  (21 other events, 428.2 us)
